TPU v7x, 32 devices: a whole 2x2x4 slice. The times are simulated.
32 devices in a mesh: dp: 8 (over y, x, core), fsdp: 4 (over z).
Axes of the slice: x: 2, y: 2, z: 4, core: 2. Of those that a mesh axis runs over, the one named last changes fastest.
Arguments:
- tokens: bfloat16 [2, 32, 512, 768], P(None, ('dp', 'fsdp')), may hold values from -6 to 6
- cotangent: bfloat16 [2, 32, 512, 768], P(None, ('dp', 'fsdp')), may hold values from -6 to 6
- doc_start: int32 [2, 32, 512], P(None, ('dp', 'fsdp')), may hold values 0 or 1
- memory_init: float32 [32, 512, 768], P(('dp', 'fsdp')), may hold values from -6 to 6
- norm1_gain: bfloat16 [768], P(('dp', 'fsdp')), may hold values from 0.25 to 1.75
- norm1_bias: bfloat16 [768], P(('dp', 'fsdp')), may hold values from -3 to 3
- qkv_weight: bfloat16 [768, 2304], P(('dp', 'fsdp')), may hold values from -0.21875 to 0.21875
- query_bias: bfloat16 [768], P(('dp', 'fsdp')), may hold values from -3 to 3
- value_bias: bfloat16 [768], P(('dp', 'fsdp')), may hold values from -3 to 3
- out_weight: bfloat16 [768, 768], P(('dp', 'fsdp')), may hold values from -1.75 to 1.75
- out_bias: bfloat16 [768], P(('dp', 'fsdp')), may hold values from -3 to 3
- norm2_gain: bfloat16 [768], P(('dp', 'fsdp')), may hold values from 0.25 to 1.75
- norm2_bias: bfloat16 [768], P(('dp', 'fsdp')), may hold values from -3 to 3
- up_weight: bfloat16 [768, 3072], P(('dp', 'fsdp')), may hold values from -0.21875 to 0.21875
- up_bias: bfloat16 [3072], P(('dp', 'fsdp')), may hold values from -3 to 3
- down_weight: bfloat16 [3072, 768], P(('dp', 'fsdp')), may hold values from -0.109375 to 0.109375
- down_bias: bfloat16 [768], P(('dp', 'fsdp')), may hold values from -3 to 3
Outputs:
- block_output: bfloat16 [2, 32, 512, 768], P(None, ('dp', 'fsdp'))
- tokens_grad: bfloat16 [2, 32, 512, 768], P(None, ('dp', 'fsdp'))
- norm1_gain_grad: float32 [768], P(('dp', 'fsdp'))
- norm1_bias_grad: float32 [768], P(('dp', 'fsdp'))
- qkv_weight_grad: float32 [768, 2304], P(('dp', 'fsdp'))
- query_bias_grad: float32 [768], P(('dp', 'fsdp'))
- value_bias_grad: float32 [768], P(('dp', 'fsdp'))
- out_weight_grad: float32 [768, 768], P(('dp', 'fsdp'))
- out_bias_grad: float32 [768], P(('dp', 'fsdp'))
- norm2_gain_grad: float32 [768], P(('dp', 'fsdp'))
- norm2_bias_grad: float32 [768], P(('dp', 'fsdp'))
- up_weight_grad: float32 [768, 3072], P(('dp', 'fsdp'))
- up_bias_grad: float32 [3072], P(('dp', 'fsdp'))
- down_weight_grad: float32 [3072, 768], P(('dp', 'fsdp'))
- down_bias_grad: float32 [768], P(('dp', 'fsdp'))
Inputs may be any that keep to these rules, and one draw needn't show every extreme that they name: `doc_start`: 1 marks the first token of a document.
All inputs are finite; a program needn't handle non-finite values. No bound on the sum of `doc_start` on one device may be relied on, other than what follows from the above.
Results may differ from a plain program's by a relative error of at most 0.012.
Values may be sent and summed in bfloat16 or wider, within the bound.
No kernel may reach another device: no remote copies, remote signals or barrier semaphores. Data moves between devices by JAX's collectives and lax.ppermute only.
A program may use at most 320 MiB of HBM per device.

v0:
```python
import jax
import jax.numpy as jnp
from jax import lax
from jax.sharding import PartitionSpec as P

HD = 64


highest = lax.Precision.HIGHEST
epsilon = 1e-05
masked_fill = -1000000000.0


def product_high(left, right):
    return jnp.dot(left, right, precision=highest)


def product_low(left, right):
    return jnp.dot(left, right, preferred_element_type=jnp.float32)


def product_left(left, right):
    return lax.dot_general(
        left, right, (((0,), (0,)), ((), ())), preferred_element_type=jnp.float32
    )


def product_right(left, right):
    return lax.dot_general(
        left, right, (((1,), (1,)), ((), ())), preferred_element_type=jnp.float32
    )


def rbf_tables(seg_rows, basis):
    centers = (jnp.arange(basis, dtype=jnp.float32) + 0.5) / basis

    def bumps(points):
        return jnp.exp(-0.5 * jnp.square((centers[:, None] - points[None, :]) * basis))

    old_points = 0.75 * centers
    new_points = 0.75 + 0.25 * (jnp.arange(seg_rows, dtype=jnp.float32) + 0.5) / seg_rows
    phi_old = bumps(old_points)
    phi_new = bumps(new_points)
    totals = jnp.sum(phi_old, axis=1) + jnp.sum(phi_new, axis=1)
    recon = bumps(centers)
    recon = recon / jnp.sum(recon, axis=0, keepdims=True)
    carry_table = product_high(phi_old, recon.T) / totals[:, None]
    fresh_table = phi_new / totals[:, None]
    return (carry_table, fresh_table)


def build_masks(starts):
    documents = jnp.cumsum(starts)
    positions = jnp.arange(starts.shape[0])
    local_mask = (positions[None, :] <= positions[:, None]) & (
        documents[None, :] == documents[:, None]
    )
    memory_mask = documents == 0
    keep_share = jnp.where(documents[-1] == 0, 1.0, 0.0).astype(jnp.float32)
    return (local_mask, memory_mask, keep_share)


def layer_norm(values, gain, bias):
    center = values - jnp.mean(values, axis=-1, keepdims=True)
    spread = jnp.mean(center * center, axis=-1, keepdims=True)
    return center * lax.rsqrt(spread + epsilon) * gain + bias


def attention_probs(query_heads, key_rows, local_mask, memory_mask):
    scores = jnp.einsum("ihd,jhd->hij", query_heads, key_rows, preferred_element_type=jnp.float32)
    memory_cols = jnp.broadcast_to(
        memory_mask[:, None], (local_mask.shape[0], key_rows.shape[0] - local_mask.shape[1])
    )
    allowed = jnp.concatenate([local_mask, memory_cols], axis=1)
    return jax.nn.softmax(jnp.where(allowed[None], scores, masked_fill), axis=-1)


def collect(
    norm1_gain,
    norm1_bias,
    qkv_weight,
    query_bias,
    value_bias,
    out_weight,
    out_bias,
    norm2_gain,
    norm2_bias,
    up_weight,
    up_bias,
    down_weight,
    down_bias,
):
    return (
        lax.all_gather(norm1_gain, ("dp", "fsdp"), axis=0, tiled=True),
        lax.all_gather(norm1_bias, ("dp", "fsdp"), axis=0, tiled=True),
        lax.all_gather(qkv_weight, ("dp", "fsdp"), axis=0, tiled=True),
        lax.all_gather(query_bias, ("dp", "fsdp"), axis=0, tiled=True),
        lax.all_gather(value_bias, ("dp", "fsdp"), axis=0, tiled=True),
        lax.all_gather(out_weight, ("dp", "fsdp"), axis=0, tiled=True),
        lax.all_gather(out_bias, ("dp", "fsdp"), axis=0, tiled=True),
        lax.all_gather(norm2_gain, ("dp", "fsdp"), axis=0, tiled=True),
        lax.all_gather(norm2_bias, ("dp", "fsdp"), axis=0, tiled=True),
        lax.all_gather(up_weight, ("dp", "fsdp"), axis=0, tiled=True),
        lax.all_gather(up_bias, ("dp", "fsdp"), axis=0, tiled=True),
        lax.all_gather(down_weight, ("dp", "fsdp"), axis=0, tiled=True),
        lax.all_gather(down_bias, ("dp", "fsdp"), axis=0, tiled=True),
    )


def reduce_grads(grads):
    return (
        lax.psum_scatter(grads[0], ("dp", "fsdp"), scatter_dimension=0, tiled=True),
        lax.psum_scatter(grads[1], ("dp", "fsdp"), scatter_dimension=0, tiled=True),
        lax.psum_scatter(grads[2], ("dp", "fsdp"), scatter_dimension=0, tiled=True),
        lax.psum_scatter(grads[3], ("dp", "fsdp"), scatter_dimension=0, tiled=True),
        lax.psum_scatter(grads[4], ("dp", "fsdp"), scatter_dimension=0, tiled=True),
        lax.psum_scatter(grads[5], ("dp", "fsdp"), scatter_dimension=0, tiled=True),
        lax.psum_scatter(grads[6], ("dp", "fsdp"), scatter_dimension=0, tiled=True),
        lax.psum_scatter(grads[7], ("dp", "fsdp"), scatter_dimension=0, tiled=True),
        lax.psum_scatter(grads[8], ("dp", "fsdp"), scatter_dimension=0, tiled=True),
        lax.psum_scatter(grads[9], ("dp", "fsdp"), scatter_dimension=0, tiled=True),
        lax.psum_scatter(grads[10], ("dp", "fsdp"), scatter_dimension=0, tiled=True),
        lax.psum_scatter(grads[11], ("dp", "fsdp"), scatter_dimension=0, tiled=True),
        lax.psum_scatter(grads[12], ("dp", "fsdp"), scatter_dimension=0, tiled=True),
    )


def forward(tokens_f, params, memory_low, local_mask, memory_mask):
    (
        norm1_gain,
        norm1_bias,
        qkv_weight,
        query_bias,
        value_bias,
        out_weight,
        out_bias,
        norm2_gain,
        norm2_bias,
        up_weight,
        up_bias,
        down_weight,
        down_bias,
    ) = params
    rows_here = tokens_f.shape[0]
    width = tokens_f.shape[1]
    head_count = width // HD
    normed = layer_norm(tokens_f, norm1_gain.astype(jnp.float32), norm1_bias.astype(jnp.float32))
    normed_low = normed.astype(jnp.bfloat16)
    projected = product_low(normed_low, qkv_weight)
    value_shift = value_bias.astype(jnp.float32)
    queries = ((projected[:, :width] + query_bias.astype(jnp.float32)) * 0.125).astype(jnp.bfloat16)
    local_keys = projected[:, width : 2 * width].astype(jnp.bfloat16)
    local_values = (projected[:, 2 * width :] + value_shift).astype(jnp.bfloat16)
    memory_proj = product_low(memory_low, qkv_weight[:, width:])
    memory_keys = memory_proj[:, :width].astype(jnp.bfloat16)
    memory_values = (memory_proj[:, width:] + value_shift).astype(jnp.bfloat16)
    key_rows = jnp.concatenate([local_keys, memory_keys], axis=0).reshape(-1, head_count, HD)
    value_rows = jnp.concatenate([local_values, memory_values], axis=0).reshape(-1, head_count, HD)
    query_heads = queries.reshape(rows_here, head_count, HD)
    probs = attention_probs(query_heads, key_rows, local_mask, memory_mask)
    mixture = (
        jnp.einsum(
            "hij,jhd->ihd",
            probs.astype(jnp.bfloat16),
            value_rows,
            preferred_element_type=jnp.float32,
        )
        .reshape(rows_here, width)
        .astype(jnp.bfloat16)
    )
    residual = tokens_f + product_low(mixture, out_weight) + out_bias.astype(jnp.float32)
    normed2_low = layer_norm(
        residual, norm2_gain.astype(jnp.float32), norm2_bias.astype(jnp.float32)
    ).astype(jnp.bfloat16)
    up_pre = product_low(normed2_low, up_weight) + up_bias.astype(jnp.float32)
    activated = jax.nn.gelu(up_pre, approximate=True).astype(jnp.bfloat16)
    output = residual + product_low(activated, down_weight) + down_bias.astype(jnp.float32)
    saved = (
        normed,
        normed_low,
        query_heads,
        key_rows,
        value_rows,
        mixture,
        residual,
        normed2_low,
        up_pre,
        activated,
    )
    return (output.astype(jnp.bfloat16), saved)


def backward(saved, cot_low, tokens_f, params, memory_low, local_mask, memory_mask):
    (
        norm1_gain,
        norm1_bias,
        qkv_weight,
        query_bias,
        value_bias,
        out_weight,
        out_bias,
        norm2_gain,
        norm2_bias,
        up_weight,
        up_bias,
        down_weight,
        down_bias,
    ) = params
    (
        normed,
        normed_low,
        query_heads,
        key_rows,
        value_rows,
        mixture,
        residual,
        normed2_low,
        up_pre,
        activated,
    ) = saved
    rows_here = tokens_f.shape[0]
    width = tokens_f.shape[1]
    head_count = width // HD
    cot_f = cot_low.astype(jnp.float32)
    down_bias_grad = jnp.sum(cot_f, axis=0)
    down_weight_grad = product_left(activated, cot_low)
    act_grad = product_right(cot_low, down_weight)
    gelu_pull = jax.vjp(lambda inner: jax.nn.gelu(inner, approximate=True), up_pre)[1]
    up_grad = gelu_pull(act_grad)[0].astype(jnp.bfloat16)
    up_bias_grad = jnp.sum(up_grad.astype(jnp.float32), axis=0)
    up_weight_grad = product_left(normed2_low, up_grad)
    norm2_in_grad = product_right(up_grad, up_weight)
    norm2_pull = jax.vjp(
        layer_norm, residual, norm2_gain.astype(jnp.float32), norm2_bias.astype(jnp.float32)
    )[1]
    residual_part, norm2_gain_grad, norm2_bias_grad = norm2_pull(norm2_in_grad)
    residual_grad = cot_f + residual_part
    attn_grad = residual_grad.astype(jnp.bfloat16)
    out_bias_grad = jnp.sum(attn_grad.astype(jnp.float32), axis=0)
    out_weight_grad = product_left(mixture, attn_grad)
    mixture_grad = product_right(attn_grad, out_weight).astype(jnp.bfloat16)
    grad_heads = mixture_grad.reshape(rows_here, head_count, HD)
    probs = attention_probs(query_heads, key_rows, local_mask, memory_mask)
    prob_grad = jnp.einsum(
        "ihd,jhd->hij", grad_heads, value_rows, preferred_element_type=jnp.float32
    )
    value_rows_grad = jnp.einsum(
        "hij,ihd->jhd", probs.astype(jnp.bfloat16), grad_heads, preferred_element_type=jnp.float32
    ).astype(jnp.bfloat16)
    score_grad = (probs * (prob_grad - jnp.sum(prob_grad * probs, axis=-1, keepdims=True))).astype(
        jnp.bfloat16
    )
    query_grad = (
        jnp.einsum("hij,jhd->ihd", score_grad, key_rows, preferred_element_type=jnp.float32)
        .astype(jnp.bfloat16)
        .reshape(rows_here, width)
    )
    key_rows_grad = (
        jnp.einsum("hij,ihd->jhd", score_grad, query_heads, preferred_element_type=jnp.float32)
        .astype(jnp.bfloat16)
        .reshape(-1, width)
    )
    value_rows_grad = value_rows_grad.reshape(-1, width)
    scaled_query_grad = query_grad * jnp.bfloat16(0.125)
    qkv_grad = jnp.concatenate(
        [scaled_query_grad, key_rows_grad[:rows_here], value_rows_grad[:rows_here]], axis=1
    )
    memory_grad = jnp.concatenate([key_rows_grad[rows_here:], value_rows_grad[rows_here:]], axis=1)
    query_bias_grad = jnp.sum(scaled_query_grad.astype(jnp.float32), axis=0)
    value_bias_grad = jnp.sum(value_rows_grad.astype(jnp.float32), axis=0)
    local_part = product_left(normed_low, qkv_grad)
    memory_part = product_left(memory_low, memory_grad)
    qkv_weight_grad = jnp.concatenate(
        [local_part[:, :width], local_part[:, width:] + memory_part], axis=1
    )
    normed_grad = product_right(qkv_grad, qkv_weight)
    norm1_pull = jax.vjp(
        layer_norm, tokens_f, norm1_gain.astype(jnp.float32), norm1_bias.astype(jnp.float32)
    )[1]
    tokens_part, norm1_gain_grad, norm1_bias_grad = norm1_pull(normed_grad)
    tokens_grad = (residual_grad + tokens_part).astype(jnp.bfloat16)
    grads = (
        norm1_gain_grad,
        norm1_bias_grad,
        qkv_weight_grad,
        query_bias_grad,
        value_bias_grad,
        out_weight_grad,
        out_bias_grad,
        norm2_gain_grad,
        norm2_bias_grad,
        up_weight_grad,
        up_bias_grad,
        down_weight_grad,
        down_bias_grad,
    )
    return (grads, tokens_grad)


def body(
    tokens,
    cotangent,
    doc_start,
    memory_init,
    norm1_gain,
    norm1_bias,
    qkv_weight,
    query_bias,
    value_bias,
    out_weight,
    out_bias,
    norm2_gain,
    norm2_bias,
    up_weight,
    up_bias,
    down_weight,
    down_bias,
):
    carry_table, fresh_table = rbf_tables(tokens.shape[2], memory_init.shape[1])
    memory = memory_init[0]
    grad_totals = None
    outputs = []
    input_grads = []
    for batch_index in range(tokens.shape[0]):
        gathered = collect(
            norm1_gain,
            norm1_bias,
            qkv_weight,
            query_bias,
            value_bias,
            out_weight,
            out_bias,
            norm2_gain,
            norm2_bias,
            up_weight,
            up_bias,
            down_weight,
            down_bias,
        )
        local_mask, memory_mask, keep_share = build_masks(doc_start[batch_index, 0])
        tokens_f = tokens[batch_index, 0].astype(jnp.float32)
        memory_low = memory.astype(jnp.bfloat16)
        output, saved = forward(tokens_f, gathered, memory_low, local_mask, memory_mask)
        gathered = collect(
            norm1_gain,
            norm1_bias,
            qkv_weight,
            query_bias,
            value_bias,
            out_weight,
            out_bias,
            norm2_gain,
            norm2_bias,
            up_weight,
            up_bias,
            down_weight,
            down_bias,
        )
        grads, tokens_grad = backward(
            saved,
            cotangent[batch_index, 0],
            tokens_f,
            gathered,
            memory_low,
            local_mask,
            memory_mask,
        )
        if grad_totals is None:
            grad_totals = grads
        else:
            grad_totals = tuple((total + part for total, part in zip(grad_totals, grads)))
        memory = keep_share * product_high(carry_table, memory) + product_high(
            fresh_table, saved[0]
        )
        outputs.append(output)
        input_grads.append(tokens_grad)
    shards = reduce_grads(grad_totals)
    block_output = jnp.stack(outputs)[:, None]
    tokens_grad_all = jnp.stack(input_grads)[:, None]
    return (
        block_output,
        tokens_grad_all,
        shards[0],
        shards[1],
        shards[2],
        shards[3],
        shards[4],
        shards[5],
        shards[6],
        shards[7],
        shards[8],
        shards[9],
        shards[10],
        shards[11],
        shards[12],
    )


def solution(mesh):
    placed = (
        P(None, ("dp", "fsdp"), None, None),
        P(None, ("dp", "fsdp"), None, None),
        P(None, ("dp", "fsdp"), None),
        P(("dp", "fsdp"), None, None),
        P(("dp", "fsdp")),
        P(("dp", "fsdp")),
        P(("dp", "fsdp"), None),
        P(("dp", "fsdp")),
        P(("dp", "fsdp")),
        P(("dp", "fsdp"), None),
        P(("dp", "fsdp")),
        P(("dp", "fsdp")),
        P(("dp", "fsdp")),
        P(("dp", "fsdp"), None),
        P(("dp", "fsdp")),
        P(("dp", "fsdp"), None),
        P(("dp", "fsdp")),
    )
    return jax.shard_map(
        body,
        mesh=mesh,
        in_specs=placed,
        out_specs=(
            P(None, ("dp", "fsdp"), None, None),
            P(None, ("dp", "fsdp"), None, None),
            P(("dp", "fsdp")),
            P(("dp", "fsdp")),
            P(("dp", "fsdp"), None),
            P(("dp", "fsdp")),
            P(("dp", "fsdp")),
            P(("dp", "fsdp"), None),
            P(("dp", "fsdp")),
            P(("dp", "fsdp")),
            P(("dp", "fsdp")),
            P(("dp", "fsdp"), None),
            P(("dp", "fsdp")),
            P(("dp", "fsdp"), None),
            P(("dp", "fsdp")),
        ),
        check_vma=False,
    )
```

profile of v0, /device:TPU:0, one launch (start us, length us, event | category | flops | bytes accessed | tf_op | source)
XLA Modules:
  0.0 910.5 jit_solution(15361867100209056826)
XLA Ops:
  18.0 43.1 %all-reduce.19 = (bf16[768]{0:T(1024)(128)(2,1)S(1)}, bf16[768]{0:T(1024)(128)(2,1)S(1)}, bf16[768]{0:T(1024)(128)(2,1)S(1)}, bf16[768]{0:T(1024)(128)(2,1)S(1)}...) all-reduce(bf16[768]{0:T(1024)(128)(2,1)S(1)} %dynamic-update-slice, ...), channel_id=1, replica_groups=mesh['dp'=8,'fsdp'=4] {'dp','fsdp'}, use_global_device_ids=true, to_apply=%add.1 | all-reduce | flops 9216 | bytes 36864
  67.3 2.8 fusion.88
  70.1 4.2 add_convert_fusion.4
  74.3 3.2 fusion.36
  85.0 2.8 copy.64
  87.8 3.4 fusion.34
  91.3 5.3 fusion.182
  96.6 3.3 fusion.75
  102.7 2.6 pad_maximum_fusion.2
  107.9 14.0 %fusion.202 = (f32[12,512]{1,0:T(8,128)S(1)}, f32[12,512,1024]{2,1,0:T(8,128)}) fusion(pred[512,1024]{1,0:T(8,128)(4,1)} %pad_add_fusion, bf16[512,12,64]{0,2,1:T(8,128)(2,1)} %bitcast.255, bf16[1024,12,64]{0,2,1:T(8,128)(2,1)} %bitcast.251), kind=kOutput, calls=%fused_computation.280 | convolution fusion | flops 824181760 | bytes 28073984 | tf_op jit(solution)/shard_map/sub | solution.py:75
  122.0 11.8 %fusion.100 = bf16[12,64,512]{2,1,0:T(8,128)(2,1)} fusion(bf16[1024,12,64]{0,2,1:T(8,128)(2,1)} %bitcast.265, f32[12,512,1024]{2,1,0:T(8,128)} %get-tuple-element.149, f32[12,512]{1,0:T(8,128)S(1)} %get-tuple-element.148), kind=kOutput, calls=%fused_computation.165 | convolution fusion | flops 818282496 | bytes 27549696 | tf_op jit(solution)/shard_map/hij,jhd->ihd/dot_general | solution.py:162
  142.9 2.6 pad_maximum_fusion.4
  145.5 2.8 copy.65
  152.2 14.0 %fusion.200 = (f32[12,512]{1,0:T(8,128)S(1)}, f32[12,512,1024]{2,1,0:T(8,128)}) fusion(pred[512,1024]{1,0:T(8,128)(4,1)} %pad_add_fusion.1, bf16[512,12,64]{0,2,1:T(8,128)(2,1)} %bitcast.253, bf16[1024,12,64]{0,2,1:T(8,128)(2,1)} %bitcast.249), kind=kOutput, calls=%fused_computation.278 | convolution fusion | flops 824181760 | bytes 28073984 | tf_op jit(solution)/shard_map/sub | solution.py:75
  166.3 10.9 %fusion.103 = bf16[12,64,512]{2,1,0:T(8,128)(2,1)S(1)} fusion(bf16[1024,12,64]{0,2,1:T(8,128)(2,1)} %bitcast.263, f32[12,512,1024]{2,1,0:T(8,128)} %get-tuple-element.145, f32[12,512]{1,0:T(8,128)S(1)} %get-tuple-element.144), kind=kOutput, calls=%fused_computation.166 | convolution fusion | flops 818282496 | bytes 27549696 | tf_op jit(solution)/shard_map/hij,jhd->ihd/dot_general | solution.py:162
  179.6 15.3 %all-gather.9.cloned.1.call-done = bf16[768,3072]{1,0:T(8,128)(2,1)} async-done(((bf16[24,3072]{1,0:T(8,128)(2,1)}), bf16[768,3072]{1,0:T(8,128)(2,1)}) %all-gather.9.cloned.1.call-update) | async-done | bytes 4718608 | tf_op jit(solution)/shard_map/all_gather | solution.py:103
  194.9 8.3 fusion.187
  203.3 4.8 fusion.188
  208.1 51.9 %all-gather.11.cloned.1.call-done = bf16[3072,768]{1,0:T(8,128)(2,1)} async-done(((bf16[96,768]{1,0:T(8,128)(2,1)}), bf16[3072,768]{1,0:T(8,128)(2,1)}) %all-gather.11.cloned.1.call-update) | async-done | bytes 4718608 | tf_op jit(solution)/shard_map/all_gather | solution.py:105
  260.0 11.6 %convert_reduce_fusion.1 = (f32[3072]{0:T(1024)}, bf16[512,3072]{1,0:T(8,128)(2,1)S(1)}) fusion(f32[512,3072]{1,0:T(8,128)} %fusion.187, f32[3072]{0:T(1024)S(1)} %convert_element_type.247, bf16[3072,768]{1,0:T(8,128)(2,1)} %all-gather.11.cloned.1.call-done, bf16[2,1,512,768]{3,2,1,0:T(8,128)(2,1)} %param.18), kind=kOutput, calls=%fused_computation.38 | convolution fusion | flops 2452091904 | bytes 14966784 | tf_op jit(solution)/shard_map/dot_general | solution.py:29
  271.6 7.2 convert_reduce_fusion
  278.8 2.7 fusion.208
  281.6 3.8 multiply_reduce_fusion.3
  293.4 12.0 %convert_reduce_fusion.3 = (f32[12,64]{1,0:T(8,128)}, bf16[1024,12,64]{0,2,1:T(8,128)(2,1)}) fusion(bf16[512,12,64]{0,2,1:T(8,128)(2,1)} %bitcast.273, f32[12,512,1024]{2,1,0:T(8,128)} %get-tuple-element.149, f32[12,512]{1,0:T(8,128)S(1)} %get-tuple-element.148), kind=kOutput, calls=%fused_computation.54 | convolution fusion | flops 820247808 | bytes 27552768 | tf_op jit(solution)/shard_map/hij,ihd->jhd/dot_general | solution.py:247
  305.4 16.4 %multiply_reduce_fusion.1 = (f32[12,512]{1,0:T(8,128)S(1)}, f32[12,512,1024]{2,1,0:T(8,128)}) fusion(f32[12,512,1024]{2,1,0:T(8,128)} %get-tuple-element.149, f32[12,512]{1,0:T(8,128)S(1)} %get-tuple-element.148, bf16[512,12,64]{0,2,1:T(8,128)(2,1)} %bitcast.274, bf16[1024,12,64]{0,2,1:T(8,128)(2,1)S(1)} %bitcast.266), kind=kOutput, calls=%fused_computation.5 | convolution fusion | flops 824174592 | bytes 52740096 | tf_op jit(solution)/shard_map/ihd,jhd->hij/dot_general | solution.py:244
  321.8 21.4 %multiply_convert_fusion.1 = bf16[12,512,1024]{2,1,0:T(8,128)(2,1)} fusion(f32[12,512,1024]{2,1,0:T(8,128)} %get-tuple-element.154, f32[12,512]{1,0:T(8,128)S(1)} %get-tuple-element.153, f32[12,512,1024]{2,1,0:T(8,128)} %get-tuple-element.149, f32[12,512]{1,0:T(8,128)S(1)} %get-tuple-element.148), kind=kLoop, calls=%fused_computation.4 | loop fusion | flops 25165824 | bytes 62963712 | tf_op jit(solution)/shard_map/convert_element_type | solution.py:250
  343.2 10.1 %convert_reduce_fusion.11 = (f32[12,64]{1,0:T(8,128)}, bf16[12,64,512]{2,1,0:T(8,128)(2,1)}) fusion(bf16[1024,12,64]{0,2,1:T(8,128)(2,1)S(1)} %bitcast.252, bf16[12,512,1024]{2,1,0:T(8,128)(2,1)} %multiply_convert_fusion.1), kind=kOutput, calls=%fused_computation.147 | convolution fusion | flops 806878464 | bytes 14945280 | tf_op jit(solution)/shard_map/hij,jhd->ihd/dot_general | solution.py:254
  353.3 7.0 fusion.90
  364.3 11.3 %convert_reduce_fusion.2 = (f32[12,64]{1,0:T(8,128)S(1)}, bf16[1024,12,64]{0,2,1:T(8,128)(2,1)}) fusion(bf16[512,12,64]{0,2,1:T(8,128)(2,1)} %bitcast.275, f32[12,512,1024]{2,1,0:T(8,128)} %get-tuple-element.145, f32[12,512]{1,0:T(8,128)S(1)} %get-tuple-element.144), kind=kOutput, calls=%fused_computation.53 | convolution fusion | flops 820247808 | bytes 27552768 | tf_op jit(solution)/shard_map/hij,ihd->jhd/dot_general | solution.py:247
  375.7 16.8 %multiply_reduce_fusion = (f32[12,512]{1,0:T(8,128)S(1)}, f32[12,512,1024]{2,1,0:T(8,128)}) fusion(f32[12,512,1024]{2,1,0:T(8,128)} %get-tuple-element.145, f32[12,512]{1,0:T(8,128)S(1)} %get-tuple-element.144, bf16[512,12,64]{0,2,1:T(8,128)(2,1)} %bitcast.276, bf16[1024,12,64]{0,2,1:T(8,128)(2,1)} %bitcast.264), kind=kOutput, calls=%fused_computation.3 | convolution fusion | flops 824174592 | bytes 52740096 | tf_op jit(solution)/shard_map/ihd,jhd->hij/dot_general | solution.py:244
  392.4 4.3 convolution_add_fusion.2
  400.3 17.6 %multiply_convert_fusion = bf16[12,512,1024]{2,1,0:T(8,128)(2,1)S(1)} fusion(f32[12,512,1024]{2,1,0:T(8,128)} %get-tuple-element.156, f32[12,512]{1,0:T(8,128)S(1)} %get-tuple-element.155, f32[12,512,1024]{2,1,0:T(8,128)} %get-tuple-element.145, f32[12,512]{1,0:T(8,128)S(1)} %get-tuple-element.144), kind=kLoop, calls=%fused_computation.2 | loop fusion | flops 25165824 | bytes 62963712 | tf_op jit(solution)/shard_map/convert_element_type | solution.py:250
  420.3 2.8 copy-done.1
  429.4 10.1 %convert_reduce_fusion.10 = (f32[12,64]{1,0:T(8,128)S(1)}, bf16[12,64,512]{2,1,0:T(8,128)(2,1)}) fusion(bf16[1024,12,64]{0,2,1:T(8,128)(2,1)} %bitcast.250, bf16[12,512,1024]{2,1,0:T(8,128)(2,1)} %copy-done.1), kind=kOutput, calls=%fused_computation.146 | convolution fusion | flops 806878464 | bytes 14945280 | tf_op jit(solution)/shard_map/hij,jhd->ihd/dot_general | solution.py:254
  439.5 3.9 fusion.119
  449.5 3.5 maximum_add_fusion
  453.7 6.9 fusion.130
  460.7 10.2 %convolution_add_fusion = f32[3072,768]{1,0:T(8,128)} fusion(f32[3072,768]{1,0:T(8,128)S(1)} %fusion.130, bf16[2,1,512,768]{3,2,1,0:T(8,128)(2,1)S(1)} %copy-done.14, f32[512,3072]{1,0:T(8,128)} %fusion.188, f32[3072]{0:T(1024)S(1)} %copy-done.82), kind=kOutput, calls=%fused_computation.49 | convolution fusion | flops 2434007040 | bytes 25964544 | tf_op jit(solution)/shard_map/dot_general | solution.py:23
  471.6 5.5 fusion.186
  477.1 6.0 convolution_add_fusion.1
  484.2 4.9 fusion.120
  489.1 2.7 fusion.69
  493.6 41.0 %all-reduce.18 = (f32[768]{0:T(1024)S(1)}, f32[768]{0:T(1024)S(1)}, f32[768]{0:T(1024)S(1)}, f32[768]{0:T(1024)S(1)}, f32[768]{0:T(1024)S(1)}, /*index=5*/f32[76...) all-reduce(f32[768]{0:T(1024)S(1)} %add.363, ...), channel_id=2, replica_groups=mesh['dp'=8,'fsdp'=4] {'dp','fsdp'}, use_global_device_ids=true, to_apply=%region_31.32.clone | all-reduce | flops 9216 | bytes 73728
  539.9 8.9 fusion.106
  548.8 9.2 %fusion.107 = bf16[1,512,768]{2,1,0:T(8,128)(2,1)S(1)} fusion(f32[512,768]{1,0:T(8,128)S(1)} %copy-done.7, bf16[3072,768]{1,0:T(8,128)(2,1)} %all-gather.11.cloned.1.call-done, f32[768]{0:T(1024)S(1)} %convert_element_type.249, f32[512,3072]{1,0:T(8,128)} %fusion.188, f32[3072]{0:T(1024)S(1)} %copy-done.82), kind=kOutput, calls=%fused_computation.171 | convolution fusion | flops 2432827392 | bytes 13384704 | tf_op jit(solution)/shard_map/dot_general | solution.py:19
  563.4 56.7 %reduce-scatter.5.cloned.1.call-done = f32[24,2304]{1,0:T(8,128)} async-done(((f32[768,2304]{1,0:T(8,128)}), f32[24,2304]{1,0:T(8,128)}) %reduce-scatter.5.cloned.1.call-update) | async-done | bytes 221200 | tf_op jit(solution)/shard_map/reduce_scatter | solution.py:114
  620.1 141.1 %reduce-scatter.11.cloned.1.call-done = f32[96,768]{1,0:T(8,128)} async-done(((f32[3072,768]{1,0:T(8,128)}), f32[96,768]{1,0:T(8,128)}) %reduce-scatter.11.cloned.1.call-update) | async-done | bytes 294928 | tf_op jit(solution)/shard_map/reduce_scatter | solution.py:123
  761.1 142.3 %reduce-scatter.9.cloned.1.call-done = f32[24,3072]{1,0:T(8,128)} async-done(((f32[768,3072]{1,0:T(8,128)}), f32[24,3072]{1,0:T(8,128)}) %reduce-scatter.9.cloned.1.call-update) | async-done | bytes 294928 | tf_op jit(solution)/shard_map/reduce_scatter | solution.py:121
  (382 shorter events, 88.7 us)
Async XLA Ops:
  7.2 60.1 %copy-start = (f32[1,512,768]{2,1,0:T(8,128)S(1)}, f32[1,512,768]{2,1,0:T(8,128)}, u32[]{:S(2)}) copy-start(f32[1,512,768]{2,1,0:T(8,128)} %param.20) | copy-start | bytes 4718596
  7.2 7.5 copy-start.2
  7.2 67.1 %all-gather.5.cloned.1.call-start = ((), (), s32[]{:S(2)}) async-start(), calls=%async_computation.4 | async-start | bytes 3649536 | tf_op jit(solution)/shard_map/all_gather | solution.py:96
  7.9 140.3 %all-gather.7.cloned.1.call-start = ((), (), s32[]{:S(2)}) async-start(), calls=%async_computation.5 | async-start | bytes 1216512 | tf_op jit(solution)/shard_map/all_gather | solution.py:99
  8.7 186.2 %all-gather.9.cloned.1.call-start = ((), (), s32[]{:S(2)}) async-start(), calls=%async_computation.6 | async-start | bytes 4866048 | tf_op jit(solution)/shard_map/all_gather | solution.py:103
  9.4 250.5 %all-gather.11.cloned.1.call-start = ((), (), s32[]{:S(2)}) async-start(), calls=%async_computation.7 | async-start | bytes 4866048 | tf_op jit(solution)/shard_map/all_gather | solution.py:105
  10.0 553.4 %reduce-scatter.7.cloned.1.call-start = ((), (), s32[]{:S(2)}) async-start(), calls=%async_computation.9 | async-start | bytes 2433024 | tf_op jit(solution)/shard_map/reduce_scatter | solution.py:117
  14.6 64.6 %copy-start.58 = (f32[512]{0:T(512)}, f32[512]{0:T(512)S(1)}, u32[]{:S(2)}) copy-start(f32[512]{0:T(512)S(1)} %get-tuple-element.171) | copy-start | bytes 6148
  14.6 76.6 %copy-start.56 = (f32[512]{0:T(512)}, f32[512]{0:T(512)S(1)}, u32[]{:S(2)}) copy-start(f32[512]{0:T(512)S(1)} %get-tuple-element.170) | copy-start | bytes 6148
  15.8 63.4 %copy-start.63 = (f32[512]{0:T(512)}, f32[512]{0:T(512)S(1)}, u32[]{:S(2)}) copy-start(f32[512]{0:T(512)S(1)} %fusion.162) | copy-start | bytes 6148
  15.8 75.4 %copy-start.65 = (f32[512]{0:T(512)}, f32[512]{0:T(512)S(1)}, u32[]{:S(2)}) copy-start(f32[512]{0:T(512)S(1)} %fusion.164) | copy-start | bytes 6148
  61.1 30.1 %copy-start.92 = (f32[768]{0:T(1024)}, f32[768]{0:T(1024)S(1)}, u32[]{:S(2)}) copy-start(f32[768]{0:T(1024)S(1)} %convert_element_type.231) | copy-start | bytes 9220
  61.2 30.1 %copy-start.54 = (f32[768]{0:T(1024)}, f32[768]{0:T(1024)S(1)}, u32[]{:S(2)}) copy-start(f32[768]{0:T(1024)S(1)} %convert_element_type.230) | copy-start | bytes 9220
  61.2 224.2 %copy-start.48 = (f32[768]{0:T(1024)}, f32[768]{0:T(1024)S(1)}, u32[]{:S(2)}) copy-start(f32[768]{0:T(1024)S(1)} %convert_element_type.244) | copy-start | bytes 9220
  61.2 142.1 %copy-start.50 = (f32[768]{0:T(1024)}, f32[768]{0:T(1024)S(1)}, u32[]{:S(2)}) copy-start(f32[768]{0:T(1024)S(1)} %convert_element_type.245) | copy-start | bytes 9220
  61.3 210.4 %copy-start.81 = (f32[3072]{0:T(1024)}, f32[3072]{0:T(1024)S(1)}, u32[]{:S(2)}) copy-start(f32[3072]{0:T(1024)S(1)} %convert_element_type.247) | copy-start | bytes 36868
  87.7 8.8 slice-start.2
  150.8 134.6 %copy-start.71 = (f32[512]{0:T(512)}, f32[512]{0:T(512)S(1)}, u32[]{:S(2)}) copy-start(f32[512]{0:T(512)S(1)} %broadcast_multiply_fusion.2) | copy-start | bytes 6148
  166.3 10.9 %copy-start.99 = (bf16[768,768]{1,0:T(8,128)(2,1)S(1)}, bf16[768,768]{1,0:T(8,128)(2,1)}, u32[]{:S(2)}) copy-start(bf16[768,768]{1,0:T(8,128)(2,1)} %all-gather.7.cloned.1.call-done) | copy-start | bytes 3538948
  178.1 107.3 %copy-start.52 = (f32[512]{0:T(512)}, f32[512]{0:T(512)S(1)}, u32[]{:S(2)}) copy-start(f32[512]{0:T(512)S(1)} %broadcast_multiply_fusion) | copy-start | bytes 6148
  179.5 105.9 %copy-start.85 = (f32[512]{0:T(512)}, f32[512]{0:T(512)S(1)}, u32[]{:S(2)}) copy-start(f32[512]{0:T(512)S(1)} %fusion.163) | copy-start | bytes 6148
  179.6 105.9 %copy-start.60 = (f32[512]{0:T(512)}, f32[512]{0:T(512)S(1)}, u32[]{:S(2)}) copy-start(f32[512]{0:T(512)S(1)} %fusion.165) | copy-start | bytes 6148
  179.6 23.7 %copy-start.5 = (f32[512,768]{1,0:T(8,128)S(1)}, f32[512,768]{1,0:T(8,128)}, u32[]{:S(2)}) copy-start(f32[512,768]{1,0:T(8,128)} %copy-done.4) | copy-start | bytes 4718596
  194.9 8.4 copy-start.96
  260.0 11.7 %copy-start.13 = (bf16[2,1,512,768]{3,2,1,0:T(8,128)(2,1)S(1)}, bf16[2,1,512,768]{3,2,1,0:T(8,128)(2,1)}, u32[]{:S(2)}) copy-start(bf16[2,1,512,768]{3,2,1,0:T(8,128)(2,1)} %param.18) | copy-start | bytes 4718596
  260.0 11.7 %copy-start.95 = (bf16[3072,768]{1,0:T(8,128)(2,1)S(1)}, bf16[3072,768]{1,0:T(8,128)(2,1)}, u32[]{:S(2)}) copy-start(bf16[3072,768]{1,0:T(8,128)(2,1)} %all-gather.11.cloned.1.call-done) | copy-start | bytes 14155780
  260.0 11.7 %copy-start.111 = (f32[512,3072]{1,0:T(8,128)S(1)}, f32[512,3072]{1,0:T(8,128)}, u32[]{:S(2)}) copy-start(f32[512,3072]{1,0:T(8,128)} %fusion.188) | copy-start | bytes 18874372
  260.0 18.8 %slice-start.4 = ((s8[4718592]{0:T(1024)(128)(4,1)}), s8[4194304]{0:T(1024)(128)(4,1)S(1)}, s32[]{:S(2)}) async-start(s8[4718592]{0:T(1024)(128)(4,1)} %bitcast.289), calls=%async_computation.16 | async-start | bytes 8388608
  271.6 9.9 %copy-start.112 = (bf16[512,3072]{1,0:T(8,128)(2,1)}, bf16[512,3072]{1,0:T(8,128)(2,1)S(1)}, u32[]{:S(2)}) copy-start(bf16[512,3072]{1,0:T(8,128)(2,1)S(1)} %get-tuple-element.167) | copy-start | bytes 9437188
  271.6 7.2 slice-start.5
  293.4 12.0 %copy-start.38 = (bf16[1024,768]{0,1:T(8,128)(2,1)S(1)}, bf16[1024,768]{0,1:T(8,128)(2,1)}, u32[]{:S(2)}) copy-start(bf16[1024,768]{0,1:T(8,128)(2,1)} %copy.62) | copy-start | bytes 4718596
  321.8 21.4 %copy-start.16 = (bf16[1024,768]{0,1:T(8,128)(2,1)S(1)}, bf16[1024,768]{0,1:T(8,128)(2,1)}, u32[]{:S(2)}) copy-start(bf16[1024,768]{0,1:T(8,128)(2,1)} %copy.64) | copy-start | bytes 4718596
  343.2 10.1 %copy-start.24 = (bf16[512,768]{0,1:T(8,128)(2,1)S(1)}, bf16[512,768]{0,1:T(8,128)(2,1)}, u32[]{:S(2)}) copy-start(bf16[512,768]{0,1:T(8,128)(2,1)} %copy.63) | copy-start | bytes 2359300
  353.3 7.0 copy-start.33
  353.3 7.0 copy-start.101
  396.8 223.3 %reduce-scatter.5.cloned.1.call-start = ((), (), s32[]{:S(2)}) async-start(), calls=%async_computation.8 | async-start | bytes 7299072 | tf_op jit(solution)/shard_map/reduce_scatter | solution.py:114
  399.2 24.0 %copy-start.43 = (bf16[512,12,64]{0,2,1:T(8,128)(2,1)}, bf16[512,12,64]{0,2,1:T(8,128)(2,1)S(1)}, u32[]{:S(2)}) copy-start(bf16[512,12,64]{0,2,1:T(8,128)(2,1)S(1)} %get-tuple-element.128) | copy-start | bytes 2359300
  400.3 22.9 %copy-start.45 = (bf16[512,12,64]{0,2,1:T(8,128)(2,1)}, bf16[512,12,64]{0,2,1:T(8,128)(2,1)S(1)}, u32[]{:S(2)}) copy-start(bf16[512,12,64]{0,2,1:T(8,128)(2,1)S(1)} %get-tuple-element.126) | copy-start | bytes 2359300
  400.3 17.6 %copy-start.23 = (bf16[512,768]{0,1:T(8,128)(2,1)S(1)}, bf16[512,768]{0,1:T(8,128)(2,1)}, u32[]{:S(2)}) copy-start(bf16[512,768]{0,1:T(8,128)(2,1)} %copy.66) | copy-start | bytes 2359300
  429.4 10.1 %copy-start.57 = (f32[512]{0:T(512)S(1)}, f32[512]{0:T(512)}, u32[]{:S(2)}) copy-start(f32[512]{0:T(512)} %copy-done.56) | copy-start | bytes 6148
  429.4 10.1 %copy-start.66 = (f32[512]{0:T(512)S(1)}, f32[512]{0:T(512)}, u32[]{:S(2)}) copy-start(f32[512]{0:T(512)} %copy-done.65) | copy-start | bytes 6148
  453.1 308.1 %reduce-scatter.11.cloned.1.call-start = ((), (), s32[]{:S(2)}) async-start(), calls=%async_computation.11 | async-start | bytes 9732096 | tf_op jit(solution)/shard_map/reduce_scatter | solution.py:123
  453.7 7.0 copy-start.14
  470.9 432.5 %reduce-scatter.9.cloned.1.call-start = ((), (), s32[]{:S(2)}) async-start(), calls=%async_computation.10 | async-start | bytes 9732096 | tf_op jit(solution)/shard_map/reduce_scatter | solution.py:121
  539.9 8.9 copy-start.7
  548.8 10.6 %copy-start.15 = (bf16[2,1,512,768]{3,2,1,0:T(8,128)(2,1)S(1)}, bf16[2,1,512,768]{3,2,1,0:T(8,128)(2,1)}, u32[]{:S(2)}) copy-start(bf16[2,1,512,768]{3,2,1,0:T(8,128)(2,1)} %param.18) | copy-start | bytes 4718596
  548.8 10.6 %copy-start.18 = (f32[512,768]{1,0:T(8,128)S(1)}, f32[512,768]{1,0:T(8,128)}, u32[]{:S(2)}) copy-start(f32[512,768]{1,0:T(8,128)} %copy-done.17) | copy-start | bytes 4718596
  548.8 10.6 %copy-start.20 = (f32[512,768]{1,0:T(8,128)S(1)}, f32[512,768]{1,0:T(8,128)}, u32[]{:S(2)}) copy-start(f32[512,768]{1,0:T(8,128)} %copy-done.19) | copy-start | bytes 4718596
  (79 other events, 223.5 us)
Sparse Core Ops, SparseCore 0:
  10.8 63.0 all-gather.4
  76.7 52.8 all-gather.6
  132.4 62.4 all-gather.8
  197.6 62.3 all-gather.10
  396.9 97.8 reduce-scatter.6
  501.8 118.1 reduce-scatter.4
  626.5 134.5 reduce-scatter.10
  768.6 134.7 reduce-scatter.8
where the time goes:
time: 915 us; the launch traced here: 910 us
  waiting for transfers between devices  410 us (45%)
  matrix products  275 us (30%)
  blocking collectives  84.1 us (9%)
  other arithmetic  69.8 us (8%)
  local copies, waits for them, and re-layouts  54.9 us (6%)
  between operations  16.7 us (2%)
    reduce_scatter x1, waiting for transfers between devices, reduce_grads(): lax.psum_scatter(grads[9], ('dp', 'fsdp'), scatter_dimension=0, tiled=True)  142 us
    reduce_scatter x1, waiting for transfers between devices, reduce_grads(): lax.psum_scatter(grads[11], ('dp', 'fsdp'), scatter_dimension=0, tiled=True)  141 us
    unnamed x2, blocking collectives  84.1 us
    reduce_scatter x1, waiting for transfers between devices, reduce_grads(): lax.psum_scatter(grads[2], ('dp', 'fsdp'), scatter_dimension=0, tiled=True)  56.7 us
    all_gather x1, waiting for transfers between devices, collect(): lax.all_gather(down_weight, ('dp', 'fsdp'), axis=0, tiled=True)  51.9 us
    dot_general x10, matrix products, product_low(): return jnp.dot(left, right, preferred_element_type=jnp.float32)  48.8 us
    dot_general x10, matrix products, product_left(): lax.dot_general(left, right, (((0,), (0,)), ((), ())), preferred_element_...  44.6 us
    convert_element_type x2, other arithmetic, backward(): (probs * (prob_grad - jnp.sum(prob_grad * probs, axis=-1, keepdims=True))...  39 us
  transfers between devices with their start and end apart: 8, of which 5 were waited for; matrix products, arithmetic and copies ran while one was open for 27% of the time, Pallas kernels for 0%

commit v1 on v0

--- a/solution.py
+++ b/solution.py
@@ -1,6 +1,10 @@
+import functools
+
 import jax
 import jax.numpy as jnp
 from jax import lax
+from jax.experimental import pallas as pl
+from jax.experimental.pallas import tpu as pltpu
 from jax.sharding import PartitionSpec as P
 
 HD = 64
@@ -50,11 +54,10 @@
 
 
 def build_masks(starts):
-    documents = jnp.cumsum(starts)
     positions = jnp.arange(starts.shape[0])
-    local_mask = (positions[None, :] <= positions[:, None]) & (
-        documents[None, :] == documents[:, None]
-    )
+    before = positions[None, :] <= positions[:, None]
+    documents = jnp.sum(jnp.where(before, starts[None, :], 0), axis=1)
+    local_mask = before & (documents[None, :] == documents[:, None])
     memory_mask = documents == 0
     keep_share = jnp.where(documents[-1] == 0, 1.0, 0.0).astype(jnp.float32)
     return (local_mask, memory_mask, keep_share)
@@ -75,54 +78,80 @@
     return jax.nn.softmax(jnp.where(allowed[None], scores, masked_fill), axis=-1)
 
 
-def collect(
-    norm1_gain,
-    norm1_bias,
-    qkv_weight,
-    query_bias,
-    value_bias,
-    out_weight,
-    out_bias,
-    norm2_gain,
-    norm2_bias,
-    up_weight,
-    up_bias,
-    down_weight,
-    down_bias,
-):
-    return (
-        lax.all_gather(norm1_gain, ("dp", "fsdp"), axis=0, tiled=True),
-        lax.all_gather(norm1_bias, ("dp", "fsdp"), axis=0, tiled=True),
-        lax.all_gather(qkv_weight, ("dp", "fsdp"), axis=0, tiled=True),
-        lax.all_gather(query_bias, ("dp", "fsdp"), axis=0, tiled=True),
-        lax.all_gather(value_bias, ("dp", "fsdp"), axis=0, tiled=True),
-        lax.all_gather(out_weight, ("dp", "fsdp"), axis=0, tiled=True),
-        lax.all_gather(out_bias, ("dp", "fsdp"), axis=0, tiled=True),
-        lax.all_gather(norm2_gain, ("dp", "fsdp"), axis=0, tiled=True),
-        lax.all_gather(norm2_bias, ("dp", "fsdp"), axis=0, tiled=True),
-        lax.all_gather(up_weight, ("dp", "fsdp"), axis=0, tiled=True),
-        lax.all_gather(up_bias, ("dp", "fsdp"), axis=0, tiled=True),
-        lax.all_gather(down_weight, ("dp", "fsdp"), axis=0, tiled=True),
-        lax.all_gather(down_bias, ("dp", "fsdp"), axis=0, tiled=True),
-    )
-
-
-def reduce_grads(grads):
-    return (
-        lax.psum_scatter(grads[0], ("dp", "fsdp"), scatter_dimension=0, tiled=True),
-        lax.psum_scatter(grads[1], ("dp", "fsdp"), scatter_dimension=0, tiled=True),
-        lax.psum_scatter(grads[2], ("dp", "fsdp"), scatter_dimension=0, tiled=True),
-        lax.psum_scatter(grads[3], ("dp", "fsdp"), scatter_dimension=0, tiled=True),
-        lax.psum_scatter(grads[4], ("dp", "fsdp"), scatter_dimension=0, tiled=True),
-        lax.psum_scatter(grads[5], ("dp", "fsdp"), scatter_dimension=0, tiled=True),
-        lax.psum_scatter(grads[6], ("dp", "fsdp"), scatter_dimension=0, tiled=True),
-        lax.psum_scatter(grads[7], ("dp", "fsdp"), scatter_dimension=0, tiled=True),
-        lax.psum_scatter(grads[8], ("dp", "fsdp"), scatter_dimension=0, tiled=True),
-        lax.psum_scatter(grads[9], ("dp", "fsdp"), scatter_dimension=0, tiled=True),
-        lax.psum_scatter(grads[10], ("dp", "fsdp"), scatter_dimension=0, tiled=True),
-        lax.psum_scatter(grads[11], ("dp", "fsdp"), scatter_dimension=0, tiled=True),
-        lax.psum_scatter(grads[12], ("dp", "fsdp"), scatter_dimension=0, tiled=True),
-    )
+class Links:
+    def __init__(self, mesh):
+        self.across = mesh.shape["dp"] // 2
+        self.deep = mesh.shape["fsdp"]
+        self.count = self.across * 2 * self.deep
+
+    def place(self):
+        outer = lax.axis_index("dp")
+        return (outer // 2, outer % 2, lax.axis_index("fsdp"))
+
+    def swap(self, value, column=0, core=0, depth=0):
+        pairs = []
+        for device in range(self.count):
+            outer, inner = divmod(device, self.deep)
+            target = (((outer // 2) ^ column) * 2 + ((outer % 2) ^ core)) * self.deep + (
+                inner ^ depth
+            )
+            pairs.append((device, target))
+        return lax.ppermute(value, ("dp", "fsdp"), pairs)
+
+    def gather(self, shard):
+        column, core, depth = self.place()
+        pieces = [shard] + [self.swap(shard, depth=s) for s in range(1, self.deep)]
+        line = jnp.concatenate(
+            [lax.select_n(depth ^ j, *pieces) for j in range(self.deep)], axis=0
+        )
+        lines = [line] + [self.swap(line, column=s) for s in range(1, self.across)]
+        others = [self.swap(part, core=1) for part in lines]
+        return self.assemble(lines + others)
+
+    def assemble(self, parts):
+        across = self.across
+        rows, width = parts[0].shape
+
+        def kernel(*refs):
+            sources, target, sems = refs[: 2 * across], refs[2 * across], refs[2 * across + 1]
+            outer = lax.axis_index("dp")
+            copies = []
+            for k in range(2 * across):
+                s, c = k % across, k // across
+                spot = ((outer // 2) ^ s) * 2 + ((outer % 2) ^ c)
+                copies.append(pltpu.make_async_copy(sources[k], target.at[spot], sems.at[k]))
+            for copy in copies:
+                copy.start()
+            for copy in copies:
+                copy.wait()
+
+        whole = pl.pallas_call(
+            kernel,
+            out_shape=jax.ShapeDtypeStruct((2 * across, rows, width), parts[0].dtype),
+            in_specs=[pl.BlockSpec(memory_space=pl.ANY)] * (2 * across),
+            out_specs=pl.BlockSpec(memory_space=pl.ANY),
+            scratch_shapes=[pltpu.SemaphoreType.DMA((2 * across,))],
+            name="assemble",
+        )(*parts)
+        return whole.reshape(2 * across * rows, width)
+
+    def scatter(self, grads):
+        column, core, depth = self.place()
+        _, rows, width = grads.shape
+        grads = grads.reshape(self.across, 2, self.deep, rows, width)
+        pick = lambda v, i, axis: lax.dynamic_index_in_dim(v, i, axis, keepdims=False)
+        came = self.swap(pick(grads, 1 - core, 1).astype(jnp.bfloat16), core=1)
+        total = pick(grads, core, 1) + came.astype(jnp.float32)
+        came = [
+            self.swap(pick(total, column ^ s, 0).astype(jnp.bfloat16), column=s)
+            for s in range(1, self.across)
+        ]
+        total = sum((part.astype(jnp.float32) for part in came), pick(total, column, 0))
+        came = [
+            self.swap(pick(total, depth ^ s, 0).astype(jnp.bfloat16), depth=s)
+            for s in range(1, self.deep)
+        ]
+        return sum((part.astype(jnp.float32) for part in came), pick(total, depth, 0))
 
 
 def forward(tokens_f, params, memory_low, local_mask, memory_mask):
@@ -297,70 +326,73 @@
     return (grads, tokens_grad)
 
 
-def body(
-    tokens,
-    cotangent,
-    doc_start,
-    memory_init,
-    norm1_gain,
-    norm1_bias,
-    qkv_weight,
-    query_bias,
-    value_bias,
-    out_weight,
-    out_bias,
-    norm2_gain,
-    norm2_bias,
-    up_weight,
-    up_bias,
-    down_weight,
-    down_bias,
-):
+def body(links, tokens, cotangent, doc_start, memory_init, *shards):
+    (
+        norm1_gain,
+        norm1_bias,
+        qkv_weight,
+        query_bias,
+        value_bias,
+        out_weight,
+        out_bias,
+        norm2_gain,
+        norm2_bias,
+        up_weight,
+        up_bias,
+        down_weight,
+        down_bias,
+    ) = shards
+    own, width = out_weight.shape
+    hidden = up_weight.shape[1]
+    fold = hidden // width
+    n = links.count
+    small = (norm1_gain, norm1_bias, query_bias, value_bias, out_bias, norm2_gain, norm2_bias, down_bias)
+    small_row = jnp.concatenate(small + (up_bias,))
+    small_size = small_row.shape[0]
+    small_rows = jnp.zeros((8, 3 * width), jnp.bfloat16).at[0, :small_size].set(small_row)
+    first = links.gather(jnp.concatenate([qkv_weight, small_rows], axis=0))
+    first = first.reshape(n, own + 8, 3 * width)
+    qkv_full = first[:, :own].reshape(n * own, 3 * width)
+    small_all = first[:, own, :small_size]
+    vectors = [small_all[:, k * own : (k + 1) * own].reshape(width) for k in range(8)]
+    up_bias_full = small_all[:, 8 * own :].reshape(hidden)
+    second = jnp.concatenate(
+        [out_weight] + [up_weight[:, k * width : (k + 1) * width] for k in range(fold)], axis=1
+    )
+    second = links.gather(second)
+    out_full = second[:, :width]
+    up_full = second[:, width:]
+    down_full = links.gather(down_weight)
+    params = (
+        vectors[0],
+        vectors[1],
+        qkv_full,
+        vectors[2],
+        vectors[3],
+        out_full,
+        vectors[4],
+        vectors[5],
+        vectors[6],
+        up_full,
+        up_bias_full,
+        down_full,
+        vectors[7],
+    )
     carry_table, fresh_table = rbf_tables(tokens.shape[2], memory_init.shape[1])
     memory = memory_init[0]
     grad_totals = None
     outputs = []
     input_grads = []
     for batch_index in range(tokens.shape[0]):
-        gathered = collect(
-            norm1_gain,
-            norm1_bias,
-            qkv_weight,
-            query_bias,
-            value_bias,
-            out_weight,
-            out_bias,
-            norm2_gain,
-            norm2_bias,
-            up_weight,
-            up_bias,
-            down_weight,
-            down_bias,
-        )
         local_mask, memory_mask, keep_share = build_masks(doc_start[batch_index, 0])
         tokens_f = tokens[batch_index, 0].astype(jnp.float32)
         memory_low = memory.astype(jnp.bfloat16)
-        output, saved = forward(tokens_f, gathered, memory_low, local_mask, memory_mask)
-        gathered = collect(
-            norm1_gain,
-            norm1_bias,
-            qkv_weight,
-            query_bias,
-            value_bias,
-            out_weight,
-            out_bias,
-            norm2_gain,
-            norm2_bias,
-            up_weight,
-            up_bias,
-            down_weight,
-            down_bias,
-        )
+        output, saved = forward(tokens_f, params, memory_low, local_mask, memory_mask)
         grads, tokens_grad = backward(
             saved,
             cotangent[batch_index, 0],
             tokens_f,
-            gathered,
+            params,
             memory_low,
             local_mask,
             memory_mask,
@@ -369,30 +401,40 @@
             grad_totals = grads
         else:
             grad_totals = tuple((total + part for total, part in zip(grad_totals, grads)))
-        memory = keep_share * product_high(carry_table, memory) + product_high(
-            fresh_table, saved[0]
-        )
+        if batch_index + 1 < tokens.shape[0]:
+            memory = keep_share * product_high(carry_table, memory) + product_high(
+                fresh_table, saved[0]
+            )
         outputs.append(output)
         input_grads.append(tokens_grad)
-    shards = reduce_grads(grad_totals)
+    g = grad_totals
+    small_grads = [g[k].reshape(n, own) for k in (0, 1, 3, 4, 6, 7, 8, 12)] + [g[10].reshape(n, -1)]
+    small_grads = jnp.concatenate(small_grads, axis=1)
+    small_grads = jnp.pad(small_grads[:, None], ((0, 0), (0, 7), (0, 3 * width - small_size)))
+    down_grad = links.scatter(g[11].reshape(n, -1, width))
+    second_grad = links.scatter(jnp.concatenate([g[5], g[9]], axis=1).reshape(n, own, -1))
+    first_grad = links.scatter(
+        jnp.concatenate([g[2].reshape(n, own, 3 * width), small_grads], axis=1)
+    )
+    vec = [first_grad[own, k * own : (k + 1) * own] for k in range(8)]
     block_output = jnp.stack(outputs)[:, None]
     tokens_grad_all = jnp.stack(input_grads)[:, None]
     return (
         block_output,
         tokens_grad_all,
-        shards[0],
-        shards[1],
-        shards[2],
-        shards[3],
-        shards[4],
-        shards[5],
-        shards[6],
-        shards[7],
-        shards[8],
-        shards[9],
-        shards[10],
-        shards[11],
-        shards[12],
+        vec[0],
+        vec[1],
+        first_grad[:own],
+        vec[2],
+        vec[3],
+        second_grad[:, :width],
+        vec[4],
+        vec[5],
+        vec[6],
+        second_grad[:, width:],
+        first_grad[own, 8 * own : small_size],
+        down_grad,
+        vec[7],
     )
 
 
@@ -417,7 +459,7 @@
         P(("dp", "fsdp")),
     )
     return jax.shard_map(
-        body,
+        functools.partial(body, Links(mesh)),
         mesh=mesh,
         in_specs=placed,
         out_specs=(

time: 915 us -> 1080 us (1.18)
  Pallas kernels: 0 us -> 468 us
  waiting for transfers between devices: 410 us -> 99.2 us
  blocking collectives: 84.1 us -> 0 us
  starting transfers between devices: 0.32 us -> 52.7 us
  other arithmetic: 69.8 us -> 106 us
  local copies, waits for them, and re-layouts: 54.9 us -> 72.8 us
  between operations: 16.7 us -> 3.51 us
    pallas_call x0 -> x3, Pallas kernels: none -> 468 us  [assemble(): pl.pallas_call(kernel, out_shape=jax.ShapeDtypeStruct((2 * across, rows,...]
    reduce_scatter x4 -> x0, waiting for transfers between devices: 340 us -> none  [the longest x1 142 us: reduce_grads(): lax.psum_scatter(grads[9], ('dp', 'fsdp'), scatter_dimension=0, tiled=True)]
    ppermute x0 -> x51, waiting for transfers between devices: none -> 99.2 us  [swap(): return lax.ppermute(value, ('dp', 'fsdp'), pairs)]
    unnamed x2 -> x0, blocking collectives: 84.1 us -> none
    all_gather x4 -> x0, waiting for transfers between devices: 67.2 us -> none  [the longest x1 51.9 us: collect(): lax.all_gather(down_weight, ('dp', 'fsdp'), axis=0, tiled=True)]
    ppermute x0 -> x51, starting transfers between devices: none -> 52.7 us  [swap(): return lax.ppermute(value, ('dp', 'fsdp'), pairs)]
    dot_general x10, matrix products: 48.8 us -> 34.1 us  [product_low(): return jnp.dot(left, right, preferred_element_type=jnp.float32)]
    concatenate x0 -> x5, other arithmetic: none -> 13.7 us  [the longest x1 9.44 us: body(): jnp.concatenate([g[5], g[9]], axis=1).reshape(n, own, -1)]
  transfers between devices with their start and end apart: 8 -> 51, of which waited for: 5 -> 19; matrix products, arithmetic and copies ran while one was open for 27% -> 18% of each run, Pallas kernels for 0% -> 27%
where the time goes in v1:
time: 1080 us; the launch traced here: 1070 us
  Pallas kernels  468 us (43%)
  matrix products  266 us (25%)
  other arithmetic  106 us (10%)
  waiting for transfers between devices  99.2 us (9%)
  local copies, waits for them, and re-layouts  72.8 us (7%)
  starting transfers between devices  52.7 us (5%)
    pallas_call x3, Pallas kernels, assemble(): pl.pallas_call(kernel, out_shape=jax.ShapeDtypeStruct((2 * across, rows,...  468 us
    ppermute x51, waiting for transfers between devices, swap(): return lax.ppermute(value, ('dp', 'fsdp'), pairs)  99.2 us
    ppermute x51, starting transfers between devices, swap(): return lax.ppermute(value, ('dp', 'fsdp'), pairs)  52.7 us
    dot_general x10, matrix products, product_left(): lax.dot_general(left, right, (((0,), (0,)), ((), ())), preferred_element_...  45.9 us
    convert_element_type x2, other arithmetic, backward(): (probs * (prob_grad - jnp.sum(prob_grad * probs, axis=-1, keepdims=True))...  43.2 us
    dot_general x8, matrix products, product_right(): lax.dot_general(left, right, (((1,), (1,)), ((), ())), preferred_element_...  34.8 us
    dot_general x10, matrix products, product_low(): return jnp.dot(left, right, preferred_element_type=jnp.float32)  34.1 us
    dot_general x2, matrix products, backward(): jnp.einsum('ihd,jhd->hij', grad_heads, value_rows, preferred_element_type...  33.9 us
  transfers between devices with their start and end apart: 51, of which 19 were waited for; matrix products, arithmetic and copies ran while one was open for 18% of the time, Pallas kernels for 27%

profile of v1, /device:TPU:0, one launch (start us, length us, event | category | flops | bytes accessed | tf_op | source)
XLA Modules:
  0.0 1068.3 jit_solution(3119293629261804375)
XLA Ops:
  0.7 6.3 concatenate.83
  9.1 4.0 collective-permute-start.1
  47.1 6.9 collective-permute-start.10
  58.8 7.2 collective-permute-done.4.refs_2_
  73.8 144.1 %assemble.3 = bf16[8,128,2304]{2,1,0:T(8,128)(2,1)} custom-call(bf16[128,2304]{1,0:T(8,128)(2,1)} %pad_maximum_fusion.14.refs_0_, bf16[128,2304]{1,0:T(8,128)(2,1)} %collective-permute-done.3.refs_1_, bf16[128,2304]{1,0:T(8,128)(2,1)} %collective-permute-done.4.refs_2_, bf16[128,2304]{1,0:T(8,128)(2,1)} %collective-permute-done.5.refs_3_, ...), custom_call_target="tpu_custom_call" | custom-call | tf_op jit(solution)/shard_map/assemble/pallas_call | solution.py:128
  218.9 4.0 slice.281
  235.8 4.4 fusion.161
  244.5 6.2 fusion.104
  258.2 14.1 %fusion.281 = (f32[12,512]{1,0:T(8,128)S(1)}, f32[12,512,1024]{2,1,0:T(8,128)}) fusion(pred[512,1024]{1,0:T(8,128)(4,1)} %pad_add_fusion, bf16[512,12,64]{0,2,1:T(8,128)(2,1)} %bitcast.429, bf16[1024,12,64]{0,2,1:T(8,128)(2,1)} %bitcast.403), kind=kOutput, calls=%fused_computation.440 | convolution fusion | flops 824181760 | bytes 28073984 | tf_op jit(solution)/shard_map/sub | solution.py:78
  272.2 11.7 %fusion.131 = bf16[12,64,512]{2,1,0:T(8,128)(2,1)} fusion(bf16[1024,12,64]{0,2,1:T(8,128)(2,1)} %bitcast.441, f32[12,512,1024]{2,1,0:T(8,128)} %get-tuple-element.184, f32[12,512]{1,0:T(8,128)S(1)} %get-tuple-element.183), kind=kOutput, calls=%fused_computation.218 | convolution fusion | flops 818282496 | bytes 27549696 | tf_op jit(solution)/shard_map/hij,jhd->ihd/dot_general | solution.py:191
  295.4 14.3 %fusion.279 = (f32[12,512]{1,0:T(8,128)S(1)}, f32[12,512,1024]{2,1,0:T(8,128)}) fusion(pred[512,1024]{1,0:T(8,128)(4,1)} %pad_add_fusion.1, bf16[512,12,64]{0,2,1:T(8,128)(2,1)} %bitcast.427, bf16[1024,12,64]{0,2,1:T(8,128)(2,1)} %bitcast.405), kind=kOutput, calls=%fused_computation.438 | convolution fusion | flops 824181760 | bytes 28073984 | tf_op jit(solution)/shard_map/sub | solution.py:78
  316.0 11.7 %fusion.134 = bf16[12,64,512]{2,1,0:T(8,128)(2,1)} fusion(bf16[1024,12,64]{0,2,1:T(8,128)(2,1)} %bitcast.443, f32[12,512,1024]{2,1,0:T(8,128)} %get-tuple-element.180, f32[12,512]{1,0:T(8,128)S(1)} %get-tuple-element.179), kind=kOutput, calls=%fused_computation.219 | convolution fusion | flops 818282496 | bytes 27549696 | tf_op jit(solution)/shard_map/hij,jhd->ihd/dot_general | solution.py:191
  328.8 144.1 %assemble.5 = bf16[8,384,768]{2,1,0:T(8,128)(2,1)} custom-call(bf16[384,768]{1,0:T(8,128)(2,1)} %pad_maximum_fusion.15.refs_0_, bf16[384,768]{1,0:T(8,128)(2,1)} %collective-permute-done.23.refs_1_, bf16[384,768]{1,0:T(8,128)(2,1)} %collective-permute-done.24.refs_2_, bf16[384,768]{1,0:T(8,128)(2,1)} %collective-permute-done.25.refs_3_, ...), custom_call_target="tpu_custom_call" | custom-call | tf_op jit(solution)/shard_map/assemble/pallas_call | solution.py:128
  472.9 179.9 %assemble.4 = bf16[8,96,3840]{2,1,0:T(8,128)(2,1)} custom-call(bf16[96,3840]{1,0:T(8,128)(2,1)} %pad_maximum_fusion.13.refs_0_, bf16[96,3840]{1,0:T(8,128)(2,1)} %collective-permute-done.13.refs_1_, bf16[96,3840]{1,0:T(8,128)(2,1)} %collective-permute-done.14.refs_2_, bf16[96,3840]{1,0:T(8,128)(2,1)} %collective-permute-done.15.refs_3_, ...), custom_call_target="tpu_custom_call" | custom-call | tf_op jit(solution)/shard_map/assemble/pallas_call | solution.py:128
  658.8 6.2 fusion.170
  665.1 7.4 convert_reduce_fusion.1
  672.5 5.6 fusion.267
  682.1 7.2 convert_reduce_fusion
  704.4 11.7 %convert_reduce_fusion.3 = (f32[12,64]{1,0:T(8,128)}, bf16[1024,12,64]{0,2,1:T(8,128)(2,1)}) fusion(bf16[512,12,64]{0,2,1:T(8,128)(2,1)S(1)} %bitcast.451, f32[12,512,1024]{2,1,0:T(8,128)} %get-tuple-element.184, f32[12,512]{1,0:T(8,128)S(1)} %get-tuple-element.183), kind=kOutput, calls=%fused_computation.81 | convolution fusion | flops 820247808 | bytes 27552768 | tf_op jit(solution)/shard_map/hij,ihd->jhd/dot_general | solution.py:276
  716.1 17.4 %multiply_reduce_fusion.1 = (f32[12,512]{1,0:T(8,128)S(1)}, f32[12,512,1024]{2,1,0:T(8,128)}) fusion(f32[12,512,1024]{2,1,0:T(8,128)} %get-tuple-element.184, f32[12,512]{1,0:T(8,128)S(1)} %get-tuple-element.183, bf16[512,12,64]{0,2,1:T(8,128)(2,1)S(1)} %bitcast.452, bf16[1024,12,64]{0,2,1:T(8,128)(2,1)} %bitcast.442), kind=kOutput, calls=%fused_computation.5 | convolution fusion | flops 824174592 | bytes 52740096 | tf_op jit(solution)/shard_map/ihd,jhd->hij/dot_general | solution.py:273
  733.5 21.5 %multiply_convert_fusion.1 = bf16[12,512,1024]{2,1,0:T(8,128)(2,1)} fusion(f32[12,512,1024]{2,1,0:T(8,128)} %get-tuple-element.189, f32[12,512]{1,0:T(8,128)S(1)} %get-tuple-element.188, f32[12,512,1024]{2,1,0:T(8,128)} %get-tuple-element.184, f32[12,512]{1,0:T(8,128)S(1)} %get-tuple-element.183), kind=kLoop, calls=%fused_computation.4 | loop fusion | flops 25165824 | bytes 62963712 | tf_op jit(solution)/shard_map/convert_element_type | solution.py:279
  755.0 9.5 convert_reduce_fusion.11
  764.5 8.0 fusion.119
  775.8 11.4 %convert_reduce_fusion.2 = (f32[12,64]{1,0:T(8,128)S(1)}, bf16[1024,12,64]{0,2,1:T(8,128)(2,1)}) fusion(bf16[512,12,64]{0,2,1:T(8,128)(2,1)} %bitcast.453, f32[12,512,1024]{2,1,0:T(8,128)} %get-tuple-element.180, f32[12,512]{1,0:T(8,128)S(1)} %copy-done.60), kind=kOutput, calls=%fused_computation.80 | convolution fusion | flops 820247808 | bytes 27552768 | tf_op jit(solution)/shard_map/hij,ihd->jhd/dot_general | solution.py:276
  787.1 16.5 %multiply_reduce_fusion = (f32[12,512]{1,0:T(8,128)S(1)}, f32[12,512,1024]{2,1,0:T(8,128)}) fusion(f32[12,512,1024]{2,1,0:T(8,128)} %get-tuple-element.180, f32[12,512]{1,0:T(8,128)S(1)} %copy-done.60, bf16[512,12,64]{0,2,1:T(8,128)(2,1)} %bitcast.454, bf16[1024,12,64]{0,2,1:T(8,128)(2,1)S(1)} %bitcast.444), kind=kOutput, calls=%fused_computation.3 | convolution fusion | flops 824174592 | bytes 52740096 | tf_op jit(solution)/shard_map/ihd,jhd->hij/dot_general | solution.py:273
  803.6 21.7 %multiply_convert_fusion = bf16[12,512,1024]{2,1,0:T(8,128)(2,1)} fusion(f32[12,512,1024]{2,1,0:T(8,128)} %get-tuple-element.191, f32[12,512]{1,0:T(8,128)S(1)} %get-tuple-element.190, f32[12,512,1024]{2,1,0:T(8,128)} %get-tuple-element.180, f32[12,512]{1,0:T(8,128)S(1)} %copy-done.60), kind=kLoop, calls=%fused_computation.2 | loop fusion | flops 25165824 | bytes 62963712 | tf_op jit(solution)/shard_map/convert_element_type | solution.py:279
  825.4 8.7 convert_reduce_fusion.10
  834.0 7.0 fusion.120
  846.8 5.2 fusion.154
  852.1 8.0 fusion.137
  860.2 8.8 convolution_add_fusion
  869.2 5.5 convolution_add_fusion.1
  875.3 4.4 convolution_add_fusion.2
  885.2 4.3 fusion.54
  890.0 9.4 pad_maximum_fusion
  899.4 4.7 fusion.53
  910.6 6.9 fusion.93
  922.1 4.1 slice_add_fusion.1
  938.3 4.0 fusion.138
  953.9 8.4 collective-permute-done.45
  964.0 11.9 %collective-permute-done.47 = bf16[4,96,768]{2,1,0:T(8,128)(2,1)S(1)} collective-permute-done((bf16[4,96,768]{2,1,0:T(8,128)(2,1)S(1)}, bf16[4,96,768]{2,1,0:T(8,128)(2,1)S(1)}, u32[]{:S(2)}, u32[]{:S(2)}) %collective-permute-start.47) | collective-permute-done | bytes 589856 | tf_op jit(solution)/shard_map/ppermute | solution.py:99
  979.5 8.1 collective-permute-done.31
  988.8 11.9 %collective-permute-done.33 = bf16[4,32,2304]{2,1,0:T(8,128)(2,1)S(1)} collective-permute-done((bf16[4,32,2304]{2,1,0:T(8,128)(2,1)S(1)}, bf16[4,32,2304]{2,1,0:T(8,128)(2,1)S(1)}, u32[]{:S(2)}, u32[]{:S(2)}) %collective-permute-start.33) | collective-permute-done | bytes 589856 | tf_op jit(solution)/shard_map/ppermute | solution.py:99
  1012.8 4.2 collective-permute-done.35
  1019.4 6.6 collective-permute-done.49
  1028.8 11.4 %collective-permute-done.40 = bf16[4,24,3840]{2,1,0:T(8,128)(2,1)S(1)} collective-permute-done((bf16[4,24,3840]{2,1,0:T(8,128)(2,1)S(1)}, bf16[4,24,3840]{2,1,0:T(8,128)(2,1)S(1)}, u32[]{:S(2)}, u32[]{:S(2)}) %collective-permute-start.40) | collective-permute-done | bytes 737312 | tf_op jit(solution)/shard_map/ppermute | solution.py:99
  1040.3 8.8 collective-permute-done.39
  1059.3 7.2 collective-permute-done.42
  (500 shorter events, 202.3 us)
Async XLA Ops:
  9.1 23.1 %collective-permute-start.1 = (bf16[32,2304]{1,0:T(8,128)(2,1)}, bf16[32,2304]{1,0:T(8,128)(2,1)S(1)}, u32[]{:S(2)}, u32[]{:S(2)}) collective-permute-start(bf16[32,2304]{1,0:T(8,128)(2,1)} %fusion.235), channel_id=1, source_target_pairs={{0,2},{1,3},{2,0},{3,1},{4,6},{5,7},{6,4},{7,5},{8,10},{9,11},{10,... | collective-permute-start | bytes 442376 | tf_op jit(solution)/shard_map/ppermute | solution.py:99
  13.2 20.0 %collective-permute-start.2 = (bf16[32,2304]{1,0:T(8,128)(2,1)}, bf16[32,2304]{1,0:T(8,128)(2,1)}, u32[]{:S(2)}, u32[]{:S(2)}) collective-permute-start(bf16[32,2304]{1,0:T(8,128)(2,1)} %fusion.235), channel_id=1, source_target_pairs={{0,3},{1,2},{2,1},{3,0},{4,7},{5,6},{6,5},{7,4},{8,11},{9,10},{10,... | collective-permute-start | bytes 442376 | tf_op jit(solution)/shard_map/ppermute | solution.py:99
  14.5 21.5 %collective-permute-start = (bf16[32,2304]{1,0:T(8,128)(2,1)}, bf16[32,2304]{1,0:T(8,128)(2,1)}, u32[]{:S(2)}, u32[]{:S(2)}) collective-permute-start(bf16[32,2304]{1,0:T(8,128)(2,1)} %fusion.235), channel_id=1, source_target_pairs={{0,1},{1,0},{2,3},{3,2},{4,5},{5,4},{6,7},{7,6},{8,9},{9,8},{10,11... | collective-permute-start | bytes 442376 | tf_op jit(solution)/shard_map/ppermute | solution.py:99
  14.7 26.8 %collective-permute-start.20 = (bf16[96,768]{1,0:T(8,128)(2,1)}, bf16[96,768]{1,0:T(8,128)(2,1)}, u32[]{:S(2)}, u32[]{:S(2)}) collective-permute-start(bf16[96,768]{1,0:T(8,128)(2,1)} %param.34), channel_id=1, source_target_pairs={{0,1},{1,0},{2,3},{3,2},{4,5},{5,4},{6,7},{7,6},{8,9},{9,8},{10,11... | collective-permute-start | bytes 442376 | tf_op jit(solution)/shard_map/ppermute | solution.py:99
  16.5 25.5 %collective-permute-start.21 = (bf16[96,768]{1,0:T(8,128)(2,1)}, bf16[96,768]{1,0:T(8,128)(2,1)}, u32[]{:S(2)}, u32[]{:S(2)}) collective-permute-start(bf16[96,768]{1,0:T(8,128)(2,1)} %param.34), channel_id=1, source_target_pairs={{0,2},{1,3},{2,0},{3,1},{4,6},{5,7},{6,4},{7,5},{8,10},{9,11},{10,... | collective-permute-start | bytes 442376 | tf_op jit(solution)/shard_map/ppermute | solution.py:99
  32.2 14.9 %collective-permute-start.22 = (bf16[96,768]{1,0:T(8,128)(2,1)}, bf16[96,768]{1,0:T(8,128)(2,1)}, u32[]{:S(2)}, u32[]{:S(2)}) collective-permute-start(bf16[96,768]{1,0:T(8,128)(2,1)} %param.34), channel_id=1, source_target_pairs={{0,3},{1,2},{2,1},{3,0},{4,7},{5,6},{6,5},{7,4},{8,11},{9,10},{10,... | collective-permute-start | bytes 442376 | tf_op jit(solution)/shard_map/ppermute | solution.py:99
  33.1 14.0 %collective-permute-start.12 = (bf16[24,3840]{1,0:T(8,128)(2,1)}, bf16[24,3840]{1,0:T(8,128)(2,1)}, u32[]{:S(2)}, u32[]{:S(2)}) collective-permute-start(bf16[24,3840]{1,0:T(8,128)(2,1)} %constant_dynamic-update-slice_fusion), channel_id=1, source_target_pairs={{0,3},{1,2},{2,1},{3,0},{4,7},{5,6},{6,5},{7,4},{8,11},{9,10},{10,... | collective-permute-start | bytes 552968 | tf_op jit(solution)/shard_map/ppermute | solution.py:99
  39.1 19.3 %collective-permute-start.5 = (bf16[128,2304]{1,0:T(8,128)(2,1)}, bf16[128,2304]{1,0:T(8,128)(2,1)}, u32[]{:S(2)}, u32[]{:S(2)}) collective-permute-start(bf16[128,2304]{1,0:T(8,128)(2,1)} %pad_maximum_fusion.14.refs_0_), channel_id=1, source_target_pairs={{0,24},{1,25},{2,26},{3,27},{4,28},{5,29},{6,30},{7,31},{8,16},{9,... | collective-permute-start | bytes 1769480 | tf_op jit(solution)/shard_map/ppermute | solution.py:99
  41.5 24.5 %collective-permute-start.4 = (bf16[128,2304]{1,0:T(8,128)(2,1)}, bf16[128,2304]{1,0:T(8,128)(2,1)}, u32[]{:S(2)}, u32[]{:S(2)}) collective-permute-start(bf16[128,2304]{1,0:T(8,128)(2,1)} %pad_maximum_fusion.14.refs_0_), channel_id=1, source_target_pairs={{0,16},{1,17},{2,18},{3,19},{4,20},{5,21},{6,22},{7,23},{8,24},{9,... | collective-permute-start | bytes 1769480 | tf_op jit(solution)/shard_map/ppermute | solution.py:99
  42.0 24.1 %collective-permute-start.3 = (bf16[128,2304]{1,0:T(8,128)(2,1)}, bf16[128,2304]{1,0:T(8,128)(2,1)}, u32[]{:S(2)}, u32[]{:S(2)}) collective-permute-start(bf16[128,2304]{1,0:T(8,128)(2,1)} %pad_maximum_fusion.14.refs_0_), channel_id=1, source_target_pairs={{0,8},{1,9},{2,10},{3,11},{4,12},{5,13},{6,14},{7,15},{8,0},{9,1},... | collective-permute-start | bytes 1769480 | tf_op jit(solution)/shard_map/ppermute | solution.py:99
  47.1 9.3 collective-permute-start.11
  47.1 11.2 %collective-permute-start.10 = (bf16[24,3840]{1,0:T(8,128)(2,1)}, bf16[24,3840]{1,0:T(8,128)(2,1)S(1)}, u32[]{:S(2)}, u32[]{:S(2)}) collective-permute-start(bf16[24,3840]{1,0:T(8,128)(2,1)} %constant_dynamic-update-slice_fusion), channel_id=1, source_target_pairs={{0,1},{1,0},{2,3},{3,2},{4,5},{5,4},{6,7},{7,6},{8,9},{9,8},{10,11... | collective-permute-start | bytes 552968 | tf_op jit(solution)/shard_map/ppermute | solution.py:99
  56.4 12.2 %collective-permute-start.6 = (bf16[128,2304]{1,0:T(8,128)(2,1)}, bf16[128,2304]{1,0:T(8,128)(2,1)}, u32[]{:S(2)}, u32[]{:S(2)}) collective-permute-start(bf16[128,2304]{1,0:T(8,128)(2,1)} %pad_maximum_fusion.14.refs_0_), channel_id=1, source_target_pairs={{0,4},{1,5},{2,6},{3,7},{4,0},{5,1},{6,2},{7,3},{8,12},{9,13},{10,... | collective-permute-start | bytes 1769480 | tf_op jit(solution)/shard_map/ppermute | solution.py:99
  58.3 234.8 %collective-permute-start.26 = (bf16[384,768]{1,0:T(8,128)(2,1)}, bf16[384,768]{1,0:T(8,128)(2,1)}, u32[]{:S(2)}, u32[]{:S(2)}) collective-permute-start(bf16[384,768]{1,0:T(8,128)(2,1)} %pad_maximum_fusion.15.refs_0_), channel_id=1, source_target_pairs={{0,4},{1,5},{2,6},{3,7},{4,0},{5,1},{6,2},{7,3},{8,12},{9,13},{10,... | collective-permute-start | bytes 1769480 | tf_op jit(solution)/shard_map/ppermute | solution.py:99
  58.3 12.0 %collective-permute-start.9 = (bf16[128,2304]{1,0:T(8,128)(2,1)}, bf16[128,2304]{1,0:T(8,128)(2,1)}, u32[]{:S(2)}, u32[]{:S(2)}) collective-permute-start(bf16[128,2304]{1,0:T(8,128)(2,1)} %collective-permute-done.5.refs_3_), channel_id=1, source_target_pairs={{0,4},{1,5},{2,6},{3,7},{4,0},{5,1},{6,2},{7,3},{8,12},{9,13},{10,... | collective-permute-start | bytes 1769480 | tf_op jit(solution)/shard_map/ppermute | solution.py:99
  68.6 225.8 %collective-permute-start.25 = (bf16[384,768]{1,0:T(8,128)(2,1)}, bf16[384,768]{1,0:T(8,128)(2,1)}, u32[]{:S(2)}, u32[]{:S(2)}) collective-permute-start(bf16[384,768]{1,0:T(8,128)(2,1)} %pad_maximum_fusion.15.refs_0_), channel_id=1, source_target_pairs={{0,24},{1,25},{2,26},{3,27},{4,28},{5,29},{6,30},{7,31},{8,16},{9,... | collective-permute-start | bytes 1769480 | tf_op jit(solution)/shard_map/ppermute | solution.py:99
  70.3 224.5 %collective-permute-start.24 = (bf16[384,768]{1,0:T(8,128)(2,1)}, bf16[384,768]{1,0:T(8,128)(2,1)}, u32[]{:S(2)}, u32[]{:S(2)}) collective-permute-start(bf16[384,768]{1,0:T(8,128)(2,1)} %pad_maximum_fusion.15.refs_0_), channel_id=1, source_target_pairs={{0,16},{1,17},{2,18},{3,19},{4,20},{5,21},{6,22},{7,23},{8,24},{9,... | collective-permute-start | bytes 1769480 | tf_op jit(solution)/shard_map/ppermute | solution.py:99
  71.5 223.3 %collective-permute-start.23 = (bf16[384,768]{1,0:T(8,128)(2,1)}, bf16[384,768]{1,0:T(8,128)(2,1)}, u32[]{:S(2)}, u32[]{:S(2)}) collective-permute-start(bf16[384,768]{1,0:T(8,128)(2,1)} %pad_maximum_fusion.15.refs_0_), channel_id=1, source_target_pairs={{0,8},{1,9},{2,10},{3,11},{4,12},{5,13},{6,14},{7,15},{8,0},{9,1},... | collective-permute-start | bytes 1769480 | tf_op jit(solution)/shard_map/ppermute | solution.py:99
  72.1 242.8 %collective-permute-start.15 = (bf16[96,3840]{1,0:T(8,128)(2,1)}, bf16[96,3840]{1,0:T(8,128)(2,1)}, u32[]{:S(2)}, u32[]{:S(2)}) collective-permute-start(bf16[96,3840]{1,0:T(8,128)(2,1)} %pad_maximum_fusion.13.refs_0_), channel_id=1, source_target_pairs={{0,24},{1,25},{2,26},{3,27},{4,28},{5,29},{6,30},{7,31},{8,16},{9,... | collective-permute-start | bytes 2211848 | tf_op jit(solution)/shard_map/ppermute | solution.py:99
  293.1 21.8 %collective-permute-start.14 = (bf16[96,3840]{1,0:T(8,128)(2,1)}, bf16[96,3840]{1,0:T(8,128)(2,1)}, u32[]{:S(2)}, u32[]{:S(2)}) collective-permute-start(bf16[96,3840]{1,0:T(8,128)(2,1)} %pad_maximum_fusion.13.refs_0_), channel_id=1, source_target_pairs={{0,16},{1,17},{2,18},{3,19},{4,20},{5,21},{6,22},{7,23},{8,24},{9,... | collective-permute-start | bytes 2211848 | tf_op jit(solution)/shard_map/ppermute | solution.py:99
  294.3 21.0 %collective-permute-start.13 = (bf16[96,3840]{1,0:T(8,128)(2,1)}, bf16[96,3840]{1,0:T(8,128)(2,1)}, u32[]{:S(2)}, u32[]{:S(2)}) collective-permute-start(bf16[96,3840]{1,0:T(8,128)(2,1)} %pad_maximum_fusion.13.refs_0_), channel_id=1, source_target_pairs={{0,8},{1,9},{2,10},{3,11},{4,12},{5,13},{6,14},{7,15},{8,0},{9,1},... | collective-permute-start | bytes 2211848 | tf_op jit(solution)/shard_map/ppermute | solution.py:99
  294.9 20.6 %collective-permute-start.29 = (bf16[384,768]{1,0:T(8,128)(2,1)}, bf16[384,768]{1,0:T(8,128)(2,1)}, u32[]{:S(2)}, u32[]{:S(2)}) collective-permute-start(bf16[384,768]{1,0:T(8,128)(2,1)} %collective-permute-done.25.refs_3_), channel_id=1, source_target_pairs={{0,4},{1,5},{2,6},{3,7},{4,0},{5,1},{6,2},{7,3},{8,12},{9,13},{10,... | collective-permute-start | bytes 1769480 | tf_op jit(solution)/shard_map/ppermute | solution.py:99
  294.9 21.0 %collective-permute-start.28 = (bf16[384,768]{1,0:T(8,128)(2,1)}, bf16[384,768]{1,0:T(8,128)(2,1)}, u32[]{:S(2)}, u32[]{:S(2)}) collective-permute-start(bf16[384,768]{1,0:T(8,128)(2,1)} %collective-permute-done.24.refs_2_), channel_id=1, source_target_pairs={{0,4},{1,5},{2,6},{3,7},{4,0},{5,1},{6,2},{7,3},{8,12},{9,13},{10,... | collective-permute-start | bytes 1769480 | tf_op jit(solution)/shard_map/ppermute | solution.py:99
  314.8 158.0 %collective-permute-start.16 = (bf16[96,3840]{1,0:T(8,128)(2,1)}, bf16[96,3840]{1,0:T(8,128)(2,1)}, u32[]{:S(2)}, u32[]{:S(2)}) collective-permute-start(bf16[96,3840]{1,0:T(8,128)(2,1)} %pad_maximum_fusion.13.refs_0_), channel_id=1, source_target_pairs={{0,4},{1,5},{2,6},{3,7},{4,0},{5,1},{6,2},{7,3},{8,12},{9,13},{10,... | collective-permute-start | bytes 2211848 | tf_op jit(solution)/shard_map/ppermute | solution.py:99
  314.9 13.8 %collective-permute-start.27 = (bf16[384,768]{1,0:T(8,128)(2,1)}, bf16[384,768]{1,0:T(8,128)(2,1)}, u32[]{:S(2)}, u32[]{:S(2)}) collective-permute-start(bf16[384,768]{1,0:T(8,128)(2,1)} %collective-permute-done.23.refs_1_), channel_id=1, source_target_pairs={{0,4},{1,5},{2,6},{3,7},{4,0},{5,1},{6,2},{7,3},{8,12},{9,13},{10,... | collective-permute-start | bytes 1769480 | tf_op jit(solution)/shard_map/ppermute | solution.py:99
  315.4 157.5 %collective-permute-start.19 = (bf16[96,3840]{1,0:T(8,128)(2,1)}, bf16[96,3840]{1,0:T(8,128)(2,1)}, u32[]{:S(2)}, u32[]{:S(2)}) collective-permute-start(bf16[96,3840]{1,0:T(8,128)(2,1)} %collective-permute-done.15.refs_3_), channel_id=1, source_target_pairs={{0,4},{1,5},{2,6},{3,7},{4,0},{5,1},{6,2},{7,3},{8,12},{9,13},{10,... | collective-permute-start | bytes 2211848 | tf_op jit(solution)/shard_map/ppermute | solution.py:99
  315.4 157.5 %collective-permute-start.18 = (bf16[96,3840]{1,0:T(8,128)(2,1)}, bf16[96,3840]{1,0:T(8,128)(2,1)}, u32[]{:S(2)}, u32[]{:S(2)}) collective-permute-start(bf16[96,3840]{1,0:T(8,128)(2,1)} %collective-permute-done.14.refs_2_), channel_id=1, source_target_pairs={{0,4},{1,5},{2,6},{3,7},{4,0},{5,1},{6,2},{7,3},{8,12},{9,13},{10,... | collective-permute-start | bytes 2211848 | tf_op jit(solution)/shard_map/ppermute | solution.py:99
  315.9 157.0 %collective-permute-start.17 = (bf16[96,3840]{1,0:T(8,128)(2,1)}, bf16[96,3840]{1,0:T(8,128)(2,1)}, u32[]{:S(2)}, u32[]{:S(2)}) collective-permute-start(bf16[96,3840]{1,0:T(8,128)(2,1)} %collective-permute-done.13.refs_1_), channel_id=1, source_target_pairs={{0,4},{1,5},{2,6},{3,7},{4,0},{5,1},{6,2},{7,3},{8,12},{9,13},{10,... | collective-permute-start | bytes 2211848 | tf_op jit(solution)/shard_map/ppermute | solution.py:99
  889.6 52.7 %collective-permute-start.44 = (bf16[4,4,96,768]{3,2,1,0:T(8,128)(2,1)}, bf16[4,4,96,768]{3,2,1,0:T(8,128)(2,1)}, u32[]{:S(2)}, u32[]{:S(2)}) collective-permute-start(bf16[4,4,96,768]{3,2,1,0:T(8,128)(2,1)} %fusion.54), channel_id=1, source_target_pairs={{0,4},{1,5},{2,6},{3,7},{4,0},{5,1},{6,2},{7,3},{8,12},{9,13},{10,... | collective-permute-start | bytes 7077896 | tf_op jit(solution)/shard_map/ppermute | solution.py:99
  904.1 100.3 %collective-permute-start.37 = (bf16[4,4,24,3840]{3,2,1,0:T(8,128)(2,1)}, bf16[4,4,24,3840]{3,2,1,0:T(8,128)(2,1)}, u32[]{:S(2)}, u32[]{:S(2)}) collective-permute-start(bf16[4,4,24,3840]{3,2,1,0:T(8,128)(2,1)} %fusion.53), channel_id=1, source_target_pairs={{0,4},{1,5},{2,6},{3,7},{4,0},{5,1},{6,2},{7,3},{8,12},{9,13},{10,... | collective-permute-start | bytes 8847368 | tf_op jit(solution)/shard_map/ppermute | solution.py:99
  931.8 17.9 %collective-permute-start.30 = (bf16[4,4,32,2304]{3,2,1,0:T(8,128)(2,1)S(1)}, bf16[4,4,32,2304]{3,2,1,0:T(8,128)(2,1)}, u32[]{:S(2)}, u32[]{:S(2)}) collective-permute-start(bf16[4,4,32,2304]{3,2,1,0:T(8,128)(2,1)S(1)} %fusion.55), channel_id=1, source_target_pairs={{0,4},{1,5},{2,6},{3,7},{4,0},{5,1},{6,2},{7,3},{8,12},{9,13},{10,... | collective-permute-start | bytes 7077896 | tf_op jit(solution)/shard_map/ppermute | solution.py:99
  946.1 16.2 %collective-permute-start.45 = (bf16[4,96,768]{2,1,0:T(8,128)(2,1)S(1)}, bf16[4,96,768]{2,1,0:T(8,128)(2,1)S(1)}, u32[]{:S(2)}, u32[]{:S(2)}) collective-permute-start(bf16[4,96,768]{2,1,0:T(8,128)(2,1)S(1)} %get-tuple-element.108), channel_id=1, source_target_pairs={{0,8},{1,9},{2,10},{3,11},{4,12},{5,13},{6,14},{7,15},{8,0},{9,1},... | collective-permute-start | bytes 1769480 | tf_op jit(solution)/shard_map/ppermute | solution.py:99
  947.6 28.3 %collective-permute-start.47 = (bf16[4,96,768]{2,1,0:T(8,128)(2,1)S(1)}, bf16[4,96,768]{2,1,0:T(8,128)(2,1)S(1)}, u32[]{:S(2)}, u32[]{:S(2)}) collective-permute-start(bf16[4,96,768]{2,1,0:T(8,128)(2,1)S(1)} %get-tuple-element.109), channel_id=1, source_target_pairs={{0,24},{1,25},{2,26},{3,27},{4,28},{5,29},{6,30},{7,31},{8,16},{9,... | collective-permute-start | bytes 1769480 | tf_op jit(solution)/shard_map/ppermute | solution.py:99
  949.1 29.9 %collective-permute-start.46 = (bf16[4,96,768]{2,1,0:T(8,128)(2,1)S(1)}, bf16[4,96,768]{2,1,0:T(8,128)(2,1)S(1)}, u32[]{:S(2)}, u32[]{:S(2)}) collective-permute-start(bf16[4,96,768]{2,1,0:T(8,128)(2,1)S(1)} %get-tuple-element.110), channel_id=1, source_target_pairs={{0,16},{1,17},{2,18},{3,19},{4,20},{5,21},{6,22},{7,23},{8,24},{9,... | collective-permute-start | bytes 1769480 | tf_op jit(solution)/shard_map/ppermute | solution.py:99
  952.3 35.3 %collective-permute-start.31 = (bf16[4,32,2304]{2,1,0:T(8,128)(2,1)S(1)}, bf16[4,32,2304]{2,1,0:T(8,128)(2,1)S(1)}, u32[]{:S(2)}, u32[]{:S(2)}) collective-permute-start(bf16[4,32,2304]{2,1,0:T(8,128)(2,1)S(1)} %get-tuple-element.111), channel_id=1, source_target_pairs={{0,8},{1,9},{2,10},{3,11},{4,12},{5,13},{6,14},{7,15},{8,0},{9,1},... | collective-permute-start | bytes 1769480 | tf_op jit(solution)/shard_map/ppermute | solution.py:99
  962.3 38.4 %collective-permute-start.33 = (bf16[4,32,2304]{2,1,0:T(8,128)(2,1)S(1)}, bf16[4,32,2304]{2,1,0:T(8,128)(2,1)S(1)}, u32[]{:S(2)}, u32[]{:S(2)}) collective-permute-start(bf16[4,32,2304]{2,1,0:T(8,128)(2,1)S(1)} %get-tuple-element.112), channel_id=1, source_target_pairs={{0,24},{1,25},{2,26},{3,27},{4,28},{5,29},{6,30},{7,31},{8,16},{9,... | collective-permute-start | bytes 1769480 | tf_op jit(solution)/shard_map/ppermute | solution.py:99
  975.9 26.8 %collective-permute-start.32 = (bf16[4,32,2304]{2,1,0:T(8,128)(2,1)S(1)}, bf16[4,32,2304]{2,1,0:T(8,128)(2,1)S(1)}, u32[]{:S(2)}, u32[]{:S(2)}) collective-permute-start(bf16[4,32,2304]{2,1,0:T(8,128)(2,1)S(1)} %get-tuple-element.113), channel_id=1, source_target_pairs={{0,16},{1,17},{2,18},{3,19},{4,20},{5,21},{6,22},{7,23},{8,24},{9,... | collective-permute-start | bytes 1769480 | tf_op jit(solution)/shard_map/ppermute | solution.py:99
  979.4 38.9 %collective-permute-start.48 = (bf16[96,768]{1,0:T(8,128)(2,1)S(1)}, bf16[96,768]{1,0:T(8,128)(2,1)S(1)}, u32[]{:S(2)}, u32[]{:S(2)}) collective-permute-start(bf16[96,768]{1,0:T(8,128)(2,1)S(1)} %get-tuple-element.135), channel_id=1, source_target_pairs={{0,1},{1,0},{2,3},{3,2},{4,5},{5,4},{6,7},{7,6},{8,9},{9,8},{10,11... | collective-permute-start | bytes 442376 | tf_op jit(solution)/shard_map/ppermute | solution.py:99
  987.6 31.7 %collective-permute-start.50 = (bf16[96,768]{1,0:T(8,128)(2,1)S(1)}, bf16[96,768]{1,0:T(8,128)(2,1)S(1)}, u32[]{:S(2)}, u32[]{:S(2)}) collective-permute-start(bf16[96,768]{1,0:T(8,128)(2,1)S(1)} %get-tuple-element.136), channel_id=1, source_target_pairs={{0,3},{1,2},{2,1},{3,0},{4,7},{5,6},{6,5},{7,4},{8,11},{9,10},{10,... | collective-permute-start | bytes 442376 | tf_op jit(solution)/shard_map/ppermute | solution.py:99
  1003.2 8.2 collective-permute-start.36
  1004.4 12.6 %collective-permute-start.35 = (bf16[32,2304]{1,0:T(8,128)(2,1)S(1)}, bf16[32,2304]{1,0:T(8,128)(2,1)S(1)}, u32[]{:S(2)}, u32[]{:S(2)}) collective-permute-start(bf16[32,2304]{1,0:T(8,128)(2,1)S(1)} %get-tuple-element.140), channel_id=1, source_target_pairs={{0,2},{1,3},{2,0},{3,1},{4,6},{5,7},{6,4},{7,5},{8,10},{9,11},{10,... | collective-permute-start | bytes 442376 | tf_op jit(solution)/shard_map/ppermute | solution.py:99
  1009.4 19.4 %collective-permute-start.38 = (bf16[4,24,3840]{2,1,0:T(8,128)(2,1)S(1)}, bf16[4,24,3840]{2,1,0:T(8,128)(2,1)S(1)}, u32[]{:S(2)}, u32[]{:S(2)}) collective-permute-start(bf16[4,24,3840]{2,1,0:T(8,128)(2,1)S(1)} %get-tuple-element.105), channel_id=1, source_target_pairs={{0,8},{1,9},{2,10},{3,11},{4,12},{5,13},{6,14},{7,15},{8,0},{9,1},... | collective-permute-start | bytes 2211848 | tf_op jit(solution)/shard_map/ppermute | solution.py:99
  1011.4 28.9 %collective-permute-start.40 = (bf16[4,24,3840]{2,1,0:T(8,128)(2,1)S(1)}, bf16[4,24,3840]{2,1,0:T(8,128)(2,1)S(1)}, u32[]{:S(2)}, u32[]{:S(2)}) collective-permute-start(bf16[4,24,3840]{2,1,0:T(8,128)(2,1)S(1)} %get-tuple-element.106), channel_id=1, source_target_pairs={{0,24},{1,25},{2,26},{3,27},{4,28},{5,29},{6,30},{7,31},{8,16},{9,... | collective-permute-start | bytes 2211848 | tf_op jit(solution)/shard_map/ppermute | solution.py:99
  1017.0 32.1 %collective-permute-start.39 = (bf16[4,24,3840]{2,1,0:T(8,128)(2,1)S(1)}, bf16[4,24,3840]{2,1,0:T(8,128)(2,1)S(1)}, u32[]{:S(2)}, u32[]{:S(2)}) collective-permute-start(bf16[4,24,3840]{2,1,0:T(8,128)(2,1)S(1)} %get-tuple-element.107), channel_id=1, source_target_pairs={{0,16},{1,17},{2,18},{3,19},{4,20},{5,21},{6,22},{7,23},{8,24},{9,... | collective-permute-start | bytes 2211848 | tf_op jit(solution)/shard_map/ppermute | solution.py:99
  1018.3 7.6 collective-permute-start.49
  1049.5 6.3 collective-permute-start.41
  1049.6 9.7 collective-permute-start.43
  1051.0 15.5 %collective-permute-start.42 = (bf16[24,3840]{1,0:T(8,128)(2,1)S(1)}, bf16[24,3840]{1,0:T(8,128)(2,1)S(1)}, u32[]{:S(2)}, u32[]{:S(2)}) collective-permute-start(bf16[24,3840]{1,0:T(8,128)(2,1)S(1)} %get-tuple-element.134), channel_id=1, source_target_pairs={{0,2},{1,3},{2,0},{3,1},{4,6},{5,7},{6,4},{7,5},{8,10},{9,11},{10,... | collective-permute-start | bytes 552968 | tf_op jit(solution)/shard_map/ppermute | solution.py:99
  (131 other events, 2149.8 us)
